TPU v7x, 32 devices: a whole 2x2x4 slice. The times are simulated.
32 devices in a mesh: dp: 8 (over z, x), tensor: 4 (over y, core).
Axes of the slice: x: 2, y: 2, z: 4, core: 2. Of those that a mesh axis runs over, the one named last changes fastest.
Arguments:
- block_input: bfloat16 [16, 1024, 1536], P('dp', 'tensor'), may hold values from -6 to 6
- out_grad: bfloat16 [16, 1024, 1536], P('dp', 'tensor'), may hold values from -6 to 6
- seg_lengths: int32 [16, 4], P('dp'), may hold values from 1 to 1020, as said below
- norm1_gain: bfloat16 [1536], replicated, may hold values from 0.5 to 1.5
- norm2_gain: bfloat16 [1536], replicated, may hold values from 0.5 to 1.5
- rel_bias: bfloat16 [32, 12], replicated, may hold values from -3 to 3
- w_query: bfloat16 [1536, 768], P(None, 'tensor'), may hold values from -0.078125 to 0.078125
- w_key: bfloat16 [1536, 768], P(None, 'tensor'), may hold values from -0.078125 to 0.078125
- w_value: bfloat16 [1536, 768], P(None, 'tensor'), may hold values from -0.15625 to 0.15625
- w_out: bfloat16 [768, 1536], P('tensor'), may hold values from -0.75 to 0.75
- w_gate: bfloat16 [1536, 3968], P(None, 'tensor'), may hold values from -0.15625 to 0.15625
- w_up: bfloat16 [1536, 3968], P(None, 'tensor'), may hold values from -0.15625 to 0.15625
- w_down: bfloat16 [3968, 1536], P('tensor'), may hold values from -0.09375 to 0.09375
Outputs:
- block_out: float32 [16, 1024, 1536], P('dp', 'tensor')
- input_grad: float32 [16, 1024, 1536], P('dp', 'tensor')
- norm1_grad: float32 [1536], replicated
- norm2_grad: float32 [1536], replicated
- bias_grad: float32 [32, 12], replicated
- query_grad: float32 [1536, 768], P('dp', 'tensor')
- key_grad: float32 [1536, 768], P('dp', 'tensor')
- value_grad: float32 [1536, 768], P('dp', 'tensor')
- outproj_grad: float32 [768, 1536], P('tensor', 'dp')
- gate_grad: float32 [1536, 3968], P('dp', 'tensor')
- up_grad: float32 [1536, 3968], P('dp', 'tensor')
- down_grad: float32 [3968, 1536], P('tensor', 'dp')
Inputs may be any that keep to these rules, and one draw needn't show every extreme that they name: `seg_lengths`: each row's 4 lengths add up to less than 1024; the remaining positions of the row are padding. In every row one segment covers more than three quarters of the row. In some row of every draw the longest segment has exactly 1020 positions.
All inputs are finite; a program needn't handle non-finite values.
Results may differ from a plain program's by a relative error of at most 0.014.
The roundings to bfloat16 on the way count: a program that leaves them out, or rounds other values in their place, can miss the bound.
Values may be sent and summed in bfloat16 or wider, within the bound.
No kernel may reach another device: no remote copies, remote signals or barrier semaphores. Data moves between devices by JAX's collectives and lax.ppermute only.
A program may use at most 256 MiB of HBM per device.

v0:
```python
import jax
import jax.numpy as jnp
from jax import lax
from jax.sharding import PartitionSpec as P

DK = 64


bucket_edges = (12, 16, 23, 32, 46, 64, 91)
masked_score = -1000000000.0
epsilon = 1e-06


def norm_rows(rows, gain):
    factor = lax.rsqrt(jnp.mean(rows * rows, axis=-1, keepdims=True) + epsilon)
    return rows * factor * gain


def gated_unit(gate_rows, up_rows):
    return jax.nn.gelu(gate_rows, approximate=True) * up_rows


def bucket_table(start, count, length, buckets):
    query_pos = start + jnp.arange(count, dtype=jnp.int32)
    key_pos = jnp.arange(length, dtype=jnp.int32)
    offset = key_pos[None, :] - query_pos[:, None]
    magnitude = jnp.abs(offset)
    larger = sum(((magnitude >= edge).astype(jnp.int32) for edge in bucket_edges))
    exact = buckets // 4
    inside = jnp.where(magnitude < exact, magnitude, exact + larger)
    return inside + jnp.where(offset > 0, buckets // 2, 0)


def segment_ids(lengths, length):
    ends = jnp.cumsum(lengths)
    positions = jnp.arange(length, dtype=jnp.int32)
    return jnp.sum((positions[:, None] >= ends[None, :]).astype(jnp.int32), axis=1)


def project(rows, weight):
    return jnp.einsum("rld,de->rle", rows, weight, preferred_element_type=jnp.float32)


def project_back(rows, weight):
    return jnp.einsum("rle,de->rld", rows, weight, preferred_element_type=jnp.float32)


def weight_sum(left, right):
    return jnp.einsum("rld,rle->de", left, right, preferred_element_type=jnp.float32)


def score_block(query_block, key_all, bias_block, same_block):
    raw = (
        jnp.einsum("qhd,khd->hqk", query_block, key_all, preferred_element_type=jnp.float32)
        + bias_block
    )
    return jnp.where(same_block[None], raw, masked_score)


def per_device(
    block_input,
    out_grad,
    seg_lengths,
    norm1_gain,
    norm2_gain,
    rel_bias,
    w_query,
    w_key,
    w_value,
    w_out,
    w_gate,
    w_up,
    w_down,
):
    row_count = block_input.shape[0]
    length = block_input.shape[1] * lax.axis_size("tensor")
    local_heads = w_query.shape[1] // DK
    buckets = rel_bias.shape[0]
    block_rows = min(512, length)
    blocks = length // block_rows
    gain_one = norm1_gain.astype(jnp.float32)
    gain_two = norm2_gain.astype(jnp.float32)
    first_head = lax.axis_index("tensor") * local_heads
    shard_bias_slice = lax.dynamic_slice_in_dim(rel_bias, first_head, local_heads, 1)
    bucket_indicators = []
    position_bias_blocks = []
    for block_position_index in range(blocks):
        bucket_rows = bucket_table(block_position_index * block_rows, block_rows, length, buckets)
        bucket_indicator = (
            bucket_rows[None] == jnp.arange(buckets, dtype=jnp.int32)[:, None, None]
        ).astype(jnp.bfloat16)
        bucket_indicators.append(bucket_indicator)
        position_bias_blocks.append(
            jnp.einsum(
                "mas,me->eas",
                bucket_indicator,
                shard_bias_slice,
                preferred_element_type=jnp.float32,
            )
        )
    same_masks = []
    for row_index in range(row_count):
        segids = segment_ids(seg_lengths[row_index], length)
        same_masks.append(segids[:, None] == segids[None, :])
    inputs = block_input.astype(jnp.float32)
    normed_one = norm_rows(inputs, gain_one).astype(jnp.bfloat16)
    full_one = lax.all_gather(normed_one, "tensor", axis=1, tiled=True)
    head_shape = (row_count, length, local_heads, DK)
    queries = project(full_one, w_query).astype(jnp.bfloat16).reshape(head_shape)
    key_rows = project(full_one, w_key).astype(jnp.bfloat16).reshape(head_shape)
    value_rows = project(full_one, w_value).astype(jnp.bfloat16).reshape(head_shape)
    attended_rows = []
    peaks = []
    totals = []
    for row_index in range(row_count):
        outputs = []
        for block_position_index in range(blocks):
            start = block_position_index * block_rows
            scores = score_block(
                queries[row_index, start : start + block_rows],
                key_rows[row_index],
                position_bias_blocks[block_position_index],
                same_masks[row_index][start : start + block_rows],
            )
            peak = jnp.max(scores, axis=-1, keepdims=True)
            expo = jnp.exp(scores - peak)
            total = jnp.sum(expo, axis=-1, keepdims=True)
            probs_low = (expo / total).astype(jnp.bfloat16)
            peaks.append(peak)
            totals.append(total)
            outputs.append(
                jnp.einsum(
                    "hqk,khd->qhd",
                    probs_low,
                    value_rows[row_index],
                    preferred_element_type=jnp.float32,
                )
            )
        attended_rows.append(jnp.concatenate(outputs, axis=0))
    attended = (
        jnp.stack(attended_rows).astype(jnp.bfloat16).reshape(row_count, length, local_heads * DK)
    )
    branch = lax.psum_scatter(project(attended, w_out), "tensor", scatter_dimension=1, tiled=True)
    middle = inputs + branch
    normed_two = norm_rows(middle, gain_two).astype(jnp.bfloat16)
    full_two = lax.all_gather(normed_two, "tensor", axis=1, tiled=True)
    gate_rows = project(full_two, w_gate)
    up_rows = project(full_two, w_up)
    hidden = gated_unit(gate_rows, up_rows).astype(jnp.bfloat16)
    feed_out = lax.psum_scatter(
        project(hidden, w_down).astype(jnp.bfloat16), "tensor", scatter_dimension=1, tiled=True
    ).astype(jnp.float32)
    block_out = middle + feed_out
    full_grad = lax.all_gather(out_grad, "tensor", axis=1, tiled=True)
    down_grad = weight_sum(hidden, full_grad)
    dhidden = jnp.einsum("rld,fd->rlf", full_grad, w_down, preferred_element_type=jnp.float32)
    gated_again, gated_pull = jax.vjp(gated_unit, gate_rows, up_rows)
    dgate, dup = gated_pull(dhidden)
    dgate = dgate.astype(jnp.bfloat16)
    dup = dup.astype(jnp.bfloat16)
    gate_grad = weight_sum(full_two, dgate)
    up_grad = weight_sum(full_two, dup)
    dnormed_two = lax.psum_scatter(
        project_back(dgate, w_gate) + project_back(dup, w_up),
        "tensor",
        scatter_dimension=1,
        tiled=True,
    )
    normed_again, norm_pull_two = jax.vjp(norm_rows, middle, gain_two)
    dmiddle_norm, gain_two_grad = norm_pull_two(dnormed_two)
    dmiddle = out_grad.astype(jnp.float32) + dmiddle_norm
    dbranch = dmiddle.astype(jnp.bfloat16)
    full_branch = lax.all_gather(dbranch, "tensor", axis=1, tiled=True)
    outproj_grad = jnp.einsum(
        "rle,rld->ed", attended, full_branch, preferred_element_type=jnp.float32
    )
    dattended = (
        jnp.einsum("rld,ed->rle", full_branch, w_out, preferred_element_type=jnp.float32)
        .astype(jnp.bfloat16)
        .reshape(head_shape)
    )
    bias_local_grad = jnp.zeros((buckets, local_heads), jnp.float32)
    dquery_rows = []
    dkey_rows = []
    dvalue_rows = []
    for row_index in range(row_count):
        dkey_sum = jnp.zeros((length, local_heads, DK), jnp.float32)
        value_gradient_sum = jnp.zeros((length, local_heads, DK), jnp.float32)
        dquery_parts = []
        for block_position_index in range(blocks):
            start = block_position_index * block_rows
            stored = row_index * blocks + block_position_index
            query_block = queries[row_index, start : start + block_rows]
            dout_block = dattended[row_index, start : start + block_rows]
            scores = score_block(
                query_block,
                key_rows[row_index],
                position_bias_blocks[block_position_index],
                same_masks[row_index][start : start + block_rows],
            )
            probs = jnp.exp(scores - peaks[stored]) / totals[stored]
            dprobs = jnp.einsum(
                "qhd,khd->hqk",
                dout_block,
                value_rows[row_index],
                preferred_element_type=jnp.float32,
            )
            inner = jnp.sum(probs * dprobs, axis=-1, keepdims=True)
            score_gradient = (probs * (dprobs - inner)).astype(jnp.bfloat16)
            dquery_parts.append(
                jnp.einsum(
                    "hqk,khd->qhd",
                    score_gradient,
                    key_rows[row_index],
                    preferred_element_type=jnp.float32,
                )
            )
            dkey_sum = dkey_sum + jnp.einsum(
                "hqk,qhd->khd", score_gradient, query_block, preferred_element_type=jnp.float32
            )
            value_gradient_sum = value_gradient_sum + jnp.einsum(
                "hqk,qhd->khd",
                probs.astype(jnp.bfloat16),
                dout_block,
                preferred_element_type=jnp.float32,
            )
            bias_local_grad = bias_local_grad + jnp.einsum(
                "pgl,tgl->pt",
                bucket_indicators[block_position_index],
                score_gradient,
                preferred_element_type=jnp.float32,
            )
        dquery_rows.append(jnp.concatenate(dquery_parts, axis=0))
        dkey_rows.append(dkey_sum)
        dvalue_rows.append(value_gradient_sum)
    flat_shape = (row_count, length, local_heads * DK)
    dqueries = jnp.stack(dquery_rows).astype(jnp.bfloat16).reshape(flat_shape)
    dkeys = jnp.stack(dkey_rows).astype(jnp.bfloat16).reshape(flat_shape)
    dvalues = jnp.stack(dvalue_rows).astype(jnp.bfloat16).reshape(flat_shape)
    query_grad = weight_sum(full_one, dqueries)
    key_grad = weight_sum(full_one, dkeys)
    value_grad = weight_sum(full_one, dvalues)
    query_out, key_out, value_out, gate_out, up_out, outproj_out, down_out = (
        lax.psum_scatter(query_grad, "dp", scatter_dimension=0, tiled=True),
        lax.psum_scatter(key_grad, "dp", scatter_dimension=0, tiled=True),
        lax.psum_scatter(value_grad, "dp", scatter_dimension=0, tiled=True),
        lax.psum_scatter(gate_grad, "dp", scatter_dimension=0, tiled=True),
        lax.psum_scatter(up_grad, "dp", scatter_dimension=0, tiled=True),
        lax.psum_scatter(outproj_grad, "dp", scatter_dimension=1, tiled=True),
        lax.psum_scatter(down_grad, "dp", scatter_dimension=1, tiled=True),
    )
    dnormed_one_terms = (
        project_back(dqueries, w_query)
        + project_back(dkeys, w_key)
        + project_back(dvalues, w_value)
    )
    dnormed_one = lax.psum_scatter(dnormed_one_terms, "tensor", scatter_dimension=1, tiled=True)
    normed_first, norm_pull_one = jax.vjp(norm_rows, inputs, gain_one)
    dinput_norm, gain_one_grad = norm_pull_one(dnormed_one)
    input_grad = dmiddle + dinput_norm
    bias_full = lax.dynamic_update_slice(
        jnp.zeros((buckets, rel_bias.shape[1]), jnp.float32), bias_local_grad, (0, first_head)
    )
    norm1_grad, norm2_grad, bias_grad = lax.psum(
        (gain_one_grad, gain_two_grad, bias_full), ("dp", "tensor")
    )
    return (
        block_out,
        input_grad,
        norm1_grad,
        norm2_grad,
        bias_grad,
        query_out,
        key_out,
        value_out,
        outproj_out,
        gate_out,
        up_out,
        down_out,
    )


def solution(mesh):
    in_specs = (
        P("dp", "tensor", None),
        P("dp", "tensor", None),
        P("dp", None),
        P(),
        P(),
        P(),
        P(None, "tensor"),
        P(None, "tensor"),
        P(None, "tensor"),
        P("tensor", None),
        P(None, "tensor"),
        P(None, "tensor"),
        P("tensor", None),
    )
    out_specs = (
        P("dp", "tensor", None),
        P("dp", "tensor", None),
        P(),
        P(),
        P(),
        P("dp", "tensor"),
        P("dp", "tensor"),
        P("dp", "tensor"),
        P("tensor", "dp"),
        P("dp", "tensor"),
        P("dp", "tensor"),
        P("tensor", "dp"),
    )
    return jax.shard_map(
        per_device, mesh=mesh, in_specs=in_specs, out_specs=out_specs, check_vma=False
    )
```

profile of v0, /device:TPU:0, one launch (start us, length us, event | category | flops | bytes accessed | tf_op | source)
XLA Modules:
  0.0 1415.9 jit_solution(12947845459134300601)
XLA Ops:
  20.9 11.7 fusion.6
  32.6 11.8 fusion.9
  44.4 18.9 %all-gather.5.cloned.1.call-done = bf16[2,1024,1536]{2,1,0:T(8,128)(2,1)} async-done(((bf16[2,256,1536]{2,1,0:T(8,128)(2,1)}), bf16[2,1024,1536]{2,1,0:T(8,128)(2,1)}) %all-gather.5.cloned.1.call-update) | async-done | bytes 6291472 | tf_op jit(solution)/shard_map/all_gather | solution.py:107
  168.6 98.5 %reduce-scatter.14.cloned.1.call-done = f32[2,256,1536]{2,1,0:T(8,128)} async-done(((f32[2,1024,1536]{2,1,0:T(8,128)}), f32[2,256,1536]{2,1,0:T(8,128)}) %reduce-scatter.14.cloned.1.call-update) | async-done | bytes 3145744 | tf_op jit(solution)/shard_map/reduce_scatter | solution.py:143
  273.8 45.9 %all-gather.7.cloned.1.call-done = bf16[2,1024,1536]{2,1,0:T(8,128)(2,1)} async-done(((bf16[2,256,1536]{2,1,0:T(8,128)(2,1)}), bf16[2,1024,1536]{2,1,0:T(8,128)(2,1)}) %all-gather.7.cloned.1.call-update) | async-done | bytes 6291472 | tf_op jit(solution)/shard_map/all_gather | solution.py:146
  319.7 11.9 fusion.39
  340.3 27.2 %all-gather.9.cloned.1.call-done = bf16[2,1024,1536]{2,1,0:T(8,128)(2,1)} async-done(((bf16[2,256,1536]{2,1,0:T(8,128)(2,1)}), bf16[2,1024,1536]{2,1,0:T(8,128)(2,1)}) %all-gather.9.cloned.1.call-update) | async-done | bytes 6291472 | tf_op jit(solution)/shard_map/all_gather | solution.py:154
  367.5 18.6 %multiply_convert_fusion = (bf16[2,1024,992]{1,2,0:T(8,128)(2,1)}, bf16[2,1024,992]{1,2,0:T(8,128)(2,1)}, bf16[2,1024,992]{1,2,0:T(8,128)(2,1)}) fusion(f32[2,1024,992]{1,2,0:T(8,128)} %fusion.43, f32[2,1024,992]{1,2,0:T(8,128)} %fusion.39, bf16[2,1024,1536]{2,1,0:T(8,128)(2,1)} %all-gather.9.cloned.1.call-done, bf16[992,1536]{1,0:T(8,128)(2,1)S(1)} %copy-done), kind=kOutput, calls=%fused_computation.28 | convolution fusion | flops 6293946368 | bytes 37781504 | tf_op jit(solution)/shard_map/rld,fd->rlf/dot_general | solution.py:156
  397.7 12.7 convolution_add_fusion
  410.5 99.2 %reduce-scatter.18.cloned.1.call-done = f32[2,256,1536]{2,1,0:T(8,128)} async-done(((f32[2,1024,1536]{2,1,0:T(8,128)}), f32[2,256,1536]{2,1,0:T(8,128)}) %reduce-scatter.18.cloned.1.call-update) | async-done | bytes 3145744 | tf_op jit(solution)/shard_map/reduce_scatter | solution.py:163
  518.2 46.5 %all-gather.11.cloned.1.call-done = bf16[2,1024,1536]{2,1,0:T(8,128)(2,1)} async-done(((bf16[2,256,1536]{2,1,0:T(8,128)(2,1)}), bf16[2,1024,1536]{2,1,0:T(8,128)(2,1)}) %all-gather.11.cloned.1.call-update) | async-done | bytes 6291472 | tf_op jit(solution)/shard_map/all_gather | solution.py:173
  659.0 11.7 add_add_fusion
  682.1 12.0 convolution_bitcast_fusion.2
  694.2 13.2 convolution_bitcast_fusion.1
  707.5 12.6 convolution_bitcast_fusion
  738.4 12.9 fusion.123
  762.7 12.7 fusion.141
  793.4 41.2 %all-reduce = (f32[1536]{0:T(1024)}, f32[1536]{0:T(1024)}, f32[32,12]{0,1:T(8,128)}) all-reduce(f32[1536]{0:T(1024)S(1)} %get-tuple-element.14, f32[1536]{0:T(1024)S(1)} %copy-done.52, f32[32,12]{0,1:T(8,128)S(1)} %dynamic_update_slice.3), channel_id=1, replica_groups=mesh['dp'=8,'tensor'=4] {'dp','tensor'}, use_global_device_ids=true, to_apply=%region_25.26 | all-reduce | flops 3456 | bytes 27648 | tf_op jit(solution)/shard_map/psum | solution.py:264
  848.7 114.1 %reduce-scatter.28.cloned.1.call-done = f32[192,992]{1,0:T(8,128)} async-done(((f32[1536,992]{1,0:T(8,128)}), f32[192,992]{1,0:T(8,128)}) %reduce-scatter.28.cloned.1.call-update) | async-done | bytes 761872 | tf_op jit(solution)/shard_map/reduce_scatter | solution.py:247
  962.8 121.3 %reduce-scatter.30.cloned.1.call-done = f32[192,992]{1,0:T(8,128)} async-done(((f32[1536,992]{1,0:T(8,128)}), f32[192,992]{1,0:T(8,128)}) %reduce-scatter.30.cloned.1.call-update) | async-done | bytes 761872 | tf_op jit(solution)/shard_map/reduce_scatter | solution.py:248
  1084.2 121.2 %reduce-scatter.32.cloned.1.call-done = f32[992,192]{0,1:T(8,128)} async-done(((f32[992,1536]{0,1:T(8,128)}), f32[992,192]{0,1:T(8,128)}) %reduce-scatter.32.cloned.1.call-update) | async-done | bytes 761872 | tf_op jit(solution)/shard_map/reduce_scatter | solution.py:250
  1205.3 68.1 %reduce-scatter.26.cloned.1.call-done = f32[192,192]{1,0:T(8,128)} async-done(((f32[1536,192]{1,0:T(8,128)}), f32[192,192]{1,0:T(8,128)}) %reduce-scatter.26.cloned.1.call-update) | async-done | bytes 147472 | tf_op jit(solution)/shard_map/reduce_scatter | solution.py:246
  1273.4 68.0 %reduce-scatter.24.cloned.1.call-done = f32[192,192]{1,0:T(8,128)} async-done(((f32[1536,192]{1,0:T(8,128)}), f32[192,192]{1,0:T(8,128)}) %reduce-scatter.24.cloned.1.call-update) | async-done | bytes 147472 | tf_op jit(solution)/shard_map/reduce_scatter | solution.py:245
  1341.4 67.7 %reduce-scatter.22.cloned.1.call-done = f32[192,192]{1,0:T(8,128)} async-done(((f32[1536,192]{1,0:T(8,128)}), f32[192,192]{1,0:T(8,128)}) %reduce-scatter.22.cloned.1.call-update) | async-done | bytes 147472 | tf_op jit(solution)/shard_map/reduce_scatter | solution.py:244
  (277 shorter events, 321.1 us)
Async XLA Ops:
  7.2 360.4 %copy-start = (bf16[992,1536]{1,0:T(8,128)(2,1)S(1)}, bf16[992,1536]{1,0:T(8,128)(2,1)}, u32[]{:S(2)}) copy-start(bf16[992,1536]{1,0:T(8,128)(2,1)} %param.25) | copy-start | bytes 9142276
  7.2 56.1 %all-gather.5.cloned.1.call-start = ((), (), s32[]{:S(2)}) async-start(), calls=%async_computation.11 | async-start | bytes 7864320 | tf_op jit(solution)/shard_map/all_gather | solution.py:107
  14.0 253.1 %reduce-scatter.14.cloned.1.call-start = ((), (), s32[]{:S(2)}) async-start(), calls=%async_computation.12 | async-start | bytes 15728640 | tf_op jit(solution)/shard_map/reduce_scatter | solution.py:143
  68.6 58.6 %copy-start.14 = (bf16[1,1024,192]{1,2,0:T(8,128)(2,1)}, bf16[1,1024,192]{1,2,0:T(8,128)(2,1)S(1)}, u32[]{:S(2)}) copy-start(bf16[1,1024,192]{1,2,0:T(8,128)(2,1)S(1)} %get-tuple-element.31) | copy-start | bytes 1179652
  167.9 151.8 %all-gather.7.cloned.1.call-start = ((), (), s32[]{:S(2)}) async-start(), calls=%async_computation.13 | async-start | bytes 7864320 | tf_op jit(solution)/shard_map/all_gather | solution.py:146
  168.6 345.5 %copy-start.46 = (f32[1536]{0:T(1024)}, f32[1536]{0:T(1024)S(1)}, u32[]{:S(2)}) copy-start(f32[1536]{0:T(1024)S(1)} %convert_element_type.272) | copy-start | bytes 18436
  270.0 244.1 %copy-start.50 = (f32[2,256]{1,0:T(2,128)}, f32[2,256]{1,0:T(2,128)S(1)}, u32[]{:S(2)}) copy-start(f32[2,256]{1,0:T(2,128)S(1)} %fusion.163) | copy-start | bytes 6148
  273.1 94.4 %all-gather.9.cloned.1.call-start = ((), (), s32[]{:S(2)}) async-start(), calls=%async_computation.15 | async-start | bytes 7864320 | tf_op jit(solution)/shard_map/all_gather | solution.py:154
  273.7 236.0 %reduce-scatter.18.cloned.1.call-start = ((), (), s32[]{:S(2)}) async-start(), calls=%async_computation.16 | async-start | bytes 15728640 | tf_op jit(solution)/shard_map/reduce_scatter | solution.py:163
  367.5 18.6 %copy-start.64 = (bf16[1536,992]{0,1:T(8,128)(2,1)S(1)}, bf16[1536,992]{0,1:T(8,128)(2,1)}, u32[]{:S(2)}) copy-start(bf16[1536,992]{0,1:T(8,128)(2,1)} %param.23) | copy-start | bytes 9142276
  410.5 154.2 %all-gather.11.cloned.1.call-start = ((), (), s32[]{:S(2)}) async-start(), calls=%async_computation.17 | async-start | bytes 7864320 | tf_op jit(solution)/shard_map/all_gather | solution.py:173
  518.2 268.9 %reduce-scatter.34.cloned.1.call-start = ((), (), s32[]{:S(2)}) async-start(), calls=%async_computation.25 | async-start | bytes 1769472
  613.1 175.8 %reduce-scatter.20.cloned.1.call-start = ((), (), s32[]{:S(2)}) async-start(), calls=%async_computation.18 | async-start | bytes 15728640 | tf_op jit(solution)/shard_map/reduce_scatter | solution.py:257
  670.7 170.1 %reduce-scatter.16.cloned.1.call-start = ((), (), s32[]{:S(2)}) async-start(), calls=%async_computation.14 | async-start | bytes 7864320 | tf_op jit(solution)/shard_map/reduce_scatter | solution.py:150
  682.0 280.8 %reduce-scatter.28.cloned.1.call-start = ((), (), s32[]{:S(2)}) async-start(), calls=%async_computation.22 | async-start | bytes 7077888 | tf_op jit(solution)/shard_map/reduce_scatter | solution.py:247
  694.1 390.0 %reduce-scatter.30.cloned.1.call-start = ((), (), s32[]{:S(2)}) async-start(), calls=%async_computation.23 | async-start | bytes 7077888 | tf_op jit(solution)/shard_map/reduce_scatter | solution.py:248
  707.4 497.9 %reduce-scatter.32.cloned.1.call-start = ((), (), s32[]{:S(2)}) async-start(), calls=%async_computation.24 | async-start | bytes 7077888 | tf_op jit(solution)/shard_map/reduce_scatter | solution.py:250
  720.1 553.3 %reduce-scatter.26.cloned.1.call-start = ((), (), s32[]{:S(2)}) async-start(), calls=%async_computation.21 | async-start | bytes 1769472 | tf_op jit(solution)/shard_map/reduce_scatter | solution.py:246
  726.2 615.2 %reduce-scatter.24.cloned.1.call-start = ((), (), s32[]{:S(2)}) async-start(), calls=%async_computation.20 | async-start | bytes 1769472 | tf_op jit(solution)/shard_map/reduce_scatter | solution.py:245
  732.4 676.7 %reduce-scatter.22.cloned.1.call-start = ((), (), s32[]{:S(2)}) async-start(), calls=%async_computation.19 | async-start | bytes 1769472 | tf_op jit(solution)/shard_map/reduce_scatter | solution.py:244
  775.4 59.1 %copy-start.56 = (f32[2,256]{1,0:T(2,128)S(1)}, f32[2,256]{1,0:T(2,128)}, u32[]{:S(2)}) copy-start(f32[2,256]{1,0:T(2,128)} %copy-done.55) | copy-start | bytes 6148
  775.4 65.4 %copy-start.47 = (f32[1536]{0:T(1024)S(1)}, f32[1536]{0:T(1024)}, u32[]{:S(2)}) copy-start(f32[1536]{0:T(1024)} %copy-done.46) | copy-start | bytes 18436
  775.5 65.4 %copy-start.51 = (f32[2,256]{1,0:T(2,128)S(1)}, f32[2,256]{1,0:T(2,128)}, u32[]{:S(2)}) copy-start(f32[2,256]{1,0:T(2,128)} %copy-done.50) | copy-start | bytes 6148
  775.5 65.4 %copy-start.58 = (f32[2,256]{1,0:T(2,128)S(1)}, f32[2,256]{1,0:T(2,128)}, u32[]{:S(2)}) copy-start(f32[2,256]{1,0:T(2,128)} %copy-done.57) | copy-start | bytes 6148
  (69 other events, 459.7 us)
Sparse Core Ops, SparseCore 0:
  14.1 49.0 all-gather.4
  168.1 99.0 reduce-scatter.13
  273.3 46.3 all-gather.6
  321.1 46.3 all-gather.8
  410.6 99.0 reduce-scatter.17
  518.3 46.3 all-gather.10
  613.2 64.8 reduce-scatter.33
  680.8 97.9 reduce-scatter.19
  781.5 59.2 reduce-scatter.15
  844.8 117.9 reduce-scatter.27
  967.0 117.1 reduce-scatter.29
  1088.2 117.1 reduce-scatter.31
  1209.3 64.0 reduce-scatter.25
  1277.6 63.7 reduce-scatter.23
  1345.3 63.8 reduce-scatter.21
where the time goes:
time: 1430 us; the launch traced here: 1420 us
  waiting for transfers between devices  904 us (63%)
  matrix products  376 us (26%)
  other arithmetic  65 us (5%)
  blocking collectives  41.2 us (3%)
  between operations  15.1 us (1%)
    reduce_scatter x1, waiting for transfers between devices, per_device(): lax.psum_scatter(up_grad, 'dp', scatter_dimension=0, tiled=True)  121 us
    reduce_scatter x1, waiting for transfers between devices, per_device(): lax.psum_scatter(down_grad, 'dp', scatter_dimension=1, tiled=True)  121 us
    reduce_scatter x1, waiting for transfers between devices, per_device(): lax.psum_scatter(gate_grad, 'dp', scatter_dimension=0, tiled=True)  114 us
    reduce_scatter x1, waiting for transfers between devices, per_device(): lax.psum_scatter(project_back(dgate, w_gate) + project_back(dup, w_up), '...  99.2 us
    reduce_scatter x1, waiting for transfers between devices, per_device(): lax.psum_scatter(project(attended, w_out), 'tensor', scatter_dimension=1,...  98.5 us
    reduce_scatter x1, waiting for transfers between devices, per_device(): lax.psum_scatter(value_grad, 'dp', scatter_dimension=0, tiled=True)  68.1 us
    reduce_scatter x1, waiting for transfers between devices, per_device(): lax.psum_scatter(key_grad, 'dp', scatter_dimension=0, tiled=True)  68 us
    reduce_scatter x1, waiting for transfers between devices, per_device(): lax.psum_scatter(query_grad, 'dp', scatter_dimension=0, tiled=True)  67.7 us
  transfers between devices with their start and end apart: 15, of which 13 were waited for; matrix products, arithmetic and copies ran while one was open for 17% of the time, Pallas kernels for 0%

commit v1 on v0

v1 whole, which is shorter than its diff:
```python
import functools

import jax
import jax.numpy as jnp
import numpy as np
from jax import lax
from jax.experimental import pallas as pl
from jax.experimental.pallas import tpu as pltpu
from jax.sharding import PartitionSpec as P

DK = 64
QUERY_BLOCK = 256
REACH = 128
LANES = 64
MIB = 2**20

bucket_edges = (12, 16, 23, 32, 46, 64, 91)
masked_score = -1000000000.0
epsilon = 1e-06
gelu_scale = float(np.sqrt(2 / np.pi))
gelu_cubic = 0.044715
bf16 = jnp.bfloat16
f32 = jnp.float32

across_y = ((0, 2), (2, 0), (1, 3), (3, 1))
across_core = ((0, 1), (1, 0), (2, 3), (3, 2))
across_both = ((0, 3), (3, 0), (1, 2), (2, 1))


def dot_nn(left, right):
    return lax.dot_general(left, right, (((1,), (0,)), ((), ())), preferred_element_type=f32)


def dot_nt(left, right):
    return lax.dot_general(left, right, (((1,), (1,)), ((), ())), preferred_element_type=f32)


def dot_tn(left, right):
    return lax.dot_general(left, right, (((0,), (0,)), ((), ())), preferred_element_type=f32)


def over_y(array):
    return lax.ppermute(array, "tensor", across_y)


def over_core(array):
    return lax.ppermute(array, "tensor", across_core)


def over_both(array):
    return lax.ppermute(array, "tensor", across_both)


smem = pl.BlockSpec(memory_space=pltpu.SMEM)
vmem = pl.BlockSpec(memory_space=pltpu.VMEM)
anywhere = pl.BlockSpec(memory_space=pl.ANY)


def row_of(row, shape):
    return pl.BlockSpec((1,) + shape[1:], lambda *_: (row, 0, 0))


class Order:
    def __init__(self):
        self.last = []

    def after(self, *arrays):
        self.last = self.last + list(arrays)

    def call(self, kernel, name, inputs, in_specs, outputs, room, scratch=(), out_specs=None, grid=(1,), aliases=None):
        count, extra = len(inputs), len(self.last)

        def body(*refs):
            kernel(*refs[:count], *refs[count + extra :])

        results = pl.pallas_call(
            body,
            grid=grid,
            in_specs=list(in_specs) + [anywhere] * extra,
            out_specs=out_specs or [vmem] * len(outputs),
            out_shape=[jax.ShapeDtypeStruct(shape, kind) for shape, kind in outputs],
            scratch_shapes=scratch,
            input_output_aliases=aliases or {},
            compiler_params=pltpu.CompilerParams(vmem_limit_bytes=room * MIB),
            cost_estimate=pl.CostEstimate(flops=10**13, bytes_accessed=1024, transcendentals=0),
            name=name,
        )(*inputs, *self.last)
        self.last = [results[0]]
        return results


def norm_factor(rows):
    return lax.rsqrt(jnp.mean(rows * rows, axis=-1, keepdims=True) + epsilon)


def norm_backward(dnormed, rows, gain):
    factor = norm_factor(rows)
    scaled = dnormed * gain
    return factor * (scaled - rows * factor * factor * jnp.mean(scaled * rows, axis=-1, keepdims=True))


def project_kernel(own, other_y, other_core, other_both, gain, weight_t, normed, qkv):
    count = own.shape[1]
    for index, piece in enumerate((own[0], other_y[...], other_core[0], other_both[...])):
        rows = piece.astype(f32)
        result = (rows * norm_factor(rows) * gain[...]).astype(bf16)
        at = slice(index * count, (index + 1) * count)
        normed[at, :] = result
        qkv[at, :] = dot_nt(result, weight_t[...]).astype(bf16)


def project(order, row, pieces, gain, weight_t):
    own, other_y, other_core, other_both = pieces
    count, width = other_y.shape
    return order.call(
        project_kernel,
        "normed_projections",
        (own, other_y, other_core, other_both, gain, weight_t),
        [row_of(row, own.shape), vmem, row_of(row, other_core.shape), vmem, vmem, vmem],
        [((4 * count, width), bf16), ((4 * count, weight_t.shape[0]), bf16)],
        28,
    )


def bucket_of(offset, buckets):
    magnitude = jnp.abs(offset)
    larger = sum(((magnitude >= edge).astype(jnp.int32) for edge in bucket_edges))
    exact = buckets // 4
    inside = jnp.where(magnitude < exact, magnitude, exact + larger)
    return inside + jnp.where(offset > 0, buckets // 2, 0)


def band_buckets(buckets):
    key = jnp.arange(QUERY_BLOCK + 2 * REACH, dtype=jnp.int32) - REACH
    query = jnp.arange(QUERY_BLOCK, dtype=jnp.int32)
    return bucket_of(key[:, None] - query[None, :], buckets)


def bias_parts(bias, length):
    buckets = bias.shape[0]
    index = band_buckets(buckets)
    wide = bias.astype(f32)
    band = jnp.zeros((bias.shape[1],) + index.shape, f32)
    for bucket in range(buckets):
        band = jnp.where((index == bucket)[None], wide[bucket][:, None, None], band)
    key = jnp.arange(length, dtype=jnp.int32)[:, None]
    block = jnp.arange(LANES, dtype=jnp.int32)[None]
    used = block < length // QUERY_BLOCK
    before = (key < block * QUERY_BLOCK - REACH) & used
    after = (key >= (block + 1) * QUERY_BLOCK + REACH) & used
    far_before = bias[buckets // 2 - 1][:, None, None]
    far_after = bias[buckets - 1][:, None, None]
    far = jnp.where(before[None], far_before, jnp.where(after[None], far_after, jnp.zeros((), bias.dtype)))
    return band, far


def near_keys(block, length):
    low = max(0, block * QUERY_BLOCK - REACH)
    high = min(length, (block + 1) * QUERY_BLOCK + REACH)
    return low, high, low - (block * QUERY_BLOCK - REACH)


def segment_of(position, lengths, row):
    end = jnp.int32(0)
    segment = jnp.zeros(position.shape, jnp.int32)
    for part in range(lengths.shape[1]):
        end = end + lengths[row, part]
        segment = segment + (position >= end).astype(jnp.int32)
    return segment


def fill_masks(lengths, row, masks):
    blocks, length, width = masks.shape
    key_segment = segment_of(lax.broadcasted_iota(jnp.int32, (length, width), 0), lengths, row)
    for block in range(blocks):
        at = lax.broadcasted_iota(jnp.int32, (1, width), 1) + block * width
        masks[block] = jnp.where(key_segment == segment_of(at, lengths, row), 0.0, masked_score)


def relative_block(place, block):
    along_y = jnp.bitwise_xor(place[0], block // 2)
    along_core = jnp.bitwise_xor(place[1], block % 2)
    return along_y + 2 * along_core


def rows_at(index):
    return pl.ds(pl.multiple_of(index * QUERY_BLOCK, QUERY_BLOCK), QUERY_BLOCK)


def block_scores(key_wide, query_wide, mask, band, head, block):
    length = key_wide.shape[0]
    scores = dot_nt(key_wide, query_wide) + mask
    low, high, start = near_keys(block, length)
    parts = []
    if low > 0:
        parts.append(scores[:low])
    parts.append(scores[low:high] + band[head, start : start + high - low])
    if high < length:
        parts.append(scores[high:])
    return jnp.concatenate(parts, axis=0)


def block_indicator(block):
    lane = lax.broadcasted_iota(jnp.int32, (QUERY_BLOCK, LANES), 1)
    return jnp.where(lane == block, 1.0, 0.0).astype(bf16)


def attention_forward_kernel(
    row, place, lengths, qkv, band, far, attended_keep, attended_send, logsum, masks, keys, values, attended
):
    length = qkv.shape[0]
    width = qkv.shape[1] // 3
    fill_masks(lengths, row, masks)
    blocks = length // QUERY_BLOCK
    order = [relative_block(place, block) for block in range(blocks)]
    for block in range(blocks):
        at = slice(block * QUERY_BLOCK, (block + 1) * QUERY_BLOCK)
        keys[at, :] = qkv[rows_at(order[block]), width : 2 * width]
        values[at, :] = qkv[rows_at(order[block]), 2 * width :]
    for head in range(width // DK):
        cols = slice(head * DK, (head + 1) * DK)
        key_wide = jnp.concatenate([keys[:, cols], far[head]], axis=1)
        values_t = values[:, cols].T
        for block in range(blocks):
            query_wide = jnp.concatenate([qkv[rows_at(order[block]), cols], block_indicator(block)], axis=1)
            scores = block_scores(key_wide, query_wide, masks[block], band, head, block)
            peak = jnp.max(scores, axis=0, keepdims=True)
            expo = jnp.exp(scores - peak)
            total = jnp.sum(expo, axis=0, keepdims=True)
            probs_low = (expo * (1.0 / total)).astype(bf16)
            logsum[head : head + 1, block * QUERY_BLOCK : (block + 1) * QUERY_BLOCK] = peak + jnp.log(total)
            result = dot_nn(values_t, probs_low).T.astype(bf16)
            attended[rows_at(order[block]), cols] = result
    attended_keep[...] = attended[: length // 2, :]
    attended_send[...] = attended[length // 2 :, :]


def attention_forward(order, row, place, lengths, qkv, band, far):
    length, width = qkv.shape[0], qkv.shape[1] // 3
    return order.call(
        functools.partial(attention_forward_kernel, row),
        "attention_forward",
        (place, lengths, qkv, band, far),
        [smem, smem, vmem, vmem, vmem],
        [((length // 2, width), bf16), ((length // 2, width), bf16), ((8, length), f32)],
        36,
        scratch=[
            pltpu.VMEM((length // QUERY_BLOCK, length, QUERY_BLOCK), f32),
            pltpu.VMEM((length, width), bf16),
            pltpu.VMEM((length, width), bf16),
            pltpu.VMEM((length, width), bf16),
        ],
    )


def attention_backward_kernel(
    row, place, lengths, qkv, dout_own, dout_y, dout_core, logsum, band, far, weight_t, normed,
    band_before, far_before, dqkv, dnormed_keep, dnormed_send, band_grad, far_grad, gain_sum,
    masks, keys, values, douts,
):
    length = qkv.shape[0]
    width = qkv.shape[1] // 3
    fill_masks(lengths, row, masks)
    blocks = length // QUERY_BLOCK
    order = [relative_block(place, block) for block in range(blocks)]
    for block, piece in enumerate((dout_own[...], dout_y[0], dout_core[0], dout_core[1])):
        at = slice(block * QUERY_BLOCK, (block + 1) * QUERY_BLOCK)
        keys[at, :] = qkv[rows_at(order[block]), width : 2 * width]
        values[at, :] = qkv[rows_at(order[block]), 2 * width :]
        douts[at, :] = piece
    band_grad[...] = band_before[...]
    far_grad[...] = far_before[...]
    key_at = lax.broadcasted_iota(jnp.int32, (length, LANES), 0)
    block_at = lax.broadcasted_iota(jnp.int32, (length, LANES), 1)
    before = key_at < block_at * QUERY_BLOCK - REACH
    after = key_at >= (block_at + 1) * QUERY_BLOCK + REACH
    for head in range(width // DK):
        cols = slice(head * DK, (head + 1) * DK)
        key_head = keys[:, cols]
        key_wide = jnp.concatenate([key_head, far[head]], axis=1)
        key_t = key_head.T
        value_head = values[:, cols]
        dkey_wide = None
        dvalue = None
        for block in range(blocks):
            query_wide = jnp.concatenate([qkv[rows_at(order[block]), cols], block_indicator(block)], axis=1)
            dout = douts[rows_at(order[block]), cols]
            scores = block_scores(key_wide, query_wide, masks[block], band, head, block)
            probs = jnp.exp(scores - logsum[head : head + 1, block * QUERY_BLOCK : (block + 1) * QUERY_BLOCK])
            weighted = probs * dot_nt(value_head, dout)
            inner = jnp.sum(weighted, axis=0, keepdims=True)
            dscores = (weighted - probs * inner).astype(bf16)
            dvalue_part = dot_nn(probs.astype(bf16), dout)
            dkey_part = dot_nn(dscores, query_wide)
            dvalue = dvalue_part if dvalue is None else dvalue + dvalue_part
            dkey_wide = dkey_part if dkey_wide is None else dkey_wide + dkey_part
            dqkv[rows_at(order[block]), cols] = dot_nn(key_t, dscores).T.astype(bf16)
            low, high, start = near_keys(block, length)
            band_grad[head, start : start + high - low] += dscores[low:high].astype(f32)
        for block in range(blocks):
            at = slice(block * QUERY_BLOCK, (block + 1) * QUERY_BLOCK)
            key_cols = slice(width + head * DK, width + (head + 1) * DK)
            value_cols = slice(2 * width + head * DK, 2 * width + (head + 1) * DK)
            dqkv[rows_at(order[block]), key_cols] = dkey_wide[at, :DK].astype(bf16)
            dqkv[rows_at(order[block]), value_cols] = dvalue[at].astype(bf16)
        sums = dkey_wide[:, DK:]
        far_grad[head : head + 1, :] += jnp.concatenate(
            [
                jnp.sum(jnp.where(before, sums, 0.0), axis=0, keepdims=True),
                jnp.sum(jnp.where(after, sums, 0.0), axis=0, keepdims=True),
            ],
            axis=1,
        )
    total = jnp.zeros((1, normed.shape[1]), f32)
    for half, target in enumerate((dnormed_keep, dnormed_send)):
        for part in range(2):
            at = slice((2 * half + part) * QUERY_BLOCK, (2 * half + part + 1) * QUERY_BLOCK)
            dnormed = dot_nn(dqkv[at, :], weight_t[...])
            target[part * QUERY_BLOCK : (part + 1) * QUERY_BLOCK, :] = dnormed.astype(bf16)
            total = total + jnp.sum(dnormed * normed[at, :].astype(f32), axis=0, keepdims=True)
    gain_sum[...] = total


def attention_backward(order, row, place, lengths, qkv, douts, logsum, band, far, weight_t, normed, band_before, far_before):
    length, width = qkv.shape[0], qkv.shape[1] // 3
    half = ((length // 2, normed.shape[1]), bf16)
    return order.call(
        functools.partial(attention_backward_kernel, row),
        "attention_backward",
        (place, lengths, qkv, *douts, logsum, band, far, weight_t, normed, band_before, far_before),
        [smem, smem] + [vmem] * 11,
        [(qkv.shape, bf16), half, half, (band.shape, f32), ((8, 2 * LANES), f32), ((1, normed.shape[1]), f32)],
        48,
        scratch=[
            pltpu.VMEM((length // QUERY_BLOCK, length, QUERY_BLOCK), f32),
            pltpu.VMEM((length, width), bf16),
            pltpu.VMEM((length, width), bf16),
            pltpu.VMEM((length, width), bf16),
        ],
    )


def branch_kernel(heads_0, heads_1, heads_2, heads_3, out_0, out_1, out_2, out_3, own, other_y, gain, middle, normed):
    count = own.shape[1]
    for index, piece in enumerate((own[0], other_y[...])):
        here = slice(index * count, (index + 1) * count)
        there = slice((1 - index) * count, (2 - index) * count)
        branch = (
            dot_nn(heads_0[here, :], out_0[...])
            + dot_nn(heads_1[here, :], out_1[...])
            + dot_nn(heads_2[there, :], out_2[...])
            + dot_nn(heads_3[there, :], out_3[...])
        )
        rows = piece.astype(f32) + branch
        if index == 0:
            middle[...] = rows
        normed[here, :] = (rows * norm_factor(rows) * gain[...]).astype(bf16)


def attention_branch(order, row, heads, out_parts, own, other_y, gain):
    count, width = other_y.shape
    return order.call(
        branch_kernel,
        "attention_branch",
        (*heads, *out_parts, own, other_y, gain),
        [vmem] * 8 + [row_of(row, own.shape), vmem, vmem],
        [((count, width), f32), ((2 * count, width), bf16)],
        28,
    )


def branch_backward_kernel(
    keep, received, from_y, middle, out_grad, gain, out_0, out_1, out_2, out_3,
    dmiddle, dbranch, gain_sum, douts_own, douts_core, douts_y,
):
    dnormed = summed(keep, received, from_y)
    rows = middle[...]
    result = out_grad[0].astype(f32) + norm_backward(dnormed, rows, gain[...])
    dmiddle[...] = result
    low = result.astype(bf16)
    dbranch[...] = low
    gain_sum[...] = jnp.sum(dnormed * rows * norm_factor(rows), axis=0, keepdims=True)
    douts_own[...] = dot_nt(low, out_0[...]).astype(bf16)
    douts_core[...] = dot_nt(low, out_1[...]).astype(bf16)
    douts_y[0] = dot_nt(low, out_2[...]).astype(bf16)
    douts_y[1] = dot_nt(low, out_3[...]).astype(bf16)


def branch_backward(order, row, keep, received, from_y, middle, out_grad, gain, out_parts):
    count, width = middle.shape
    first = pl.BlockSpec((count, width), lambda *_: (0, 0))
    return order.call(
        branch_backward_kernel,
        "branch_backward",
        (keep, received, from_y, middle, out_grad, gain, *out_parts),
        [first, pl.BlockSpec((1, count, width), lambda *_: (0, 0, 0)), vmem, vmem, row_of(row, out_grad.shape)]
        + [vmem] * 5,
        [((count, width), f32), ((count, width), bf16), ((1, width), f32)]
        + [((count, out_parts[0].shape[0]), bf16)] * 2
        + [((2, count, out_parts[0].shape[0]), bf16)],
        24,
    )


def outproj_grad_kernel(rows, *refs):
    heads, branches, (keep, send) = refs[: 4 * rows], refs[4 * rows : 5 * rows], refs[5 * rows :]
    count = branches[0].shape[0]
    for index in range(4):
        total = None
        for row in range(rows):
            at = slice((index // 2) * count, (index // 2 + 1) * count)
            part = dot_tn(heads[4 * row + index][at, :], branches[row][...])
            total = part if total is None else total + part
        target = keep if index % 2 == 0 else send
        target[index // 2] = total.astype(bf16)


def outproj_grad(order, heads, branches):
    rows, width, cols = len(branches), branches[0].shape[1], heads[0].shape[1]
    return order.call(
        functools.partial(outproj_grad_kernel, rows),
        "outproj_gradient",
        (*heads, *branches),
        [vmem] * (5 * rows),
        [((2, cols, width), bf16)] * 2,
        24,
    )


def load_once(sources, targets, sem):
    @pl.when(pl.program_id(0) == 0)
    def _():
        copies = [
            pltpu.make_async_copy(source, target, sem.at[index])
            for index, (source, target) in enumerate(zip(sources, targets))
        ]
        for copy in copies:
            copy.start()
        for copy in copies:
            copy.wait()


def feed_kernel(
    chunk, normed_keep, normed_recv, grad_0, grad_1, grad_2, grad_3, gate_hbm, up_hbm, down_hbm,
    hidden_ref, dgate_ref, dup_ref, dnormed_keep, feed_keep, sends, gate_t, up_t, down, sem,
):
    step = pl.program_id(0)
    load_once((gate_hbm, up_hbm, down_hbm), (gate_t, up_t, down), sem)
    normed = jnp.where(step < 2, normed_keep[...], normed_recv[...])
    grad = jnp.where(
        step < 2,
        jnp.where(step == 0, grad_0[0], grad_1[...]),
        jnp.where(step == 2, grad_2[0], grad_3[...]),
    )
    units = down.shape[0]
    for start in range(0, units, chunk):
        at = slice(start, min(units, start + chunk))
        gate = dot_nt(normed, gate_t[at, :])
        up = dot_nt(normed, up_t[at, :])
        dhidden = dot_nt(grad, down[at, :])
        square = gate * gate
        bend = jnp.tanh(gelu_scale * gate * (1.0 + gelu_cubic * square))
        half = 0.5 * (1.0 + bend)
        active = gate * half
        slope = half + (0.5 * gelu_scale) * gate * (1.0 - bend * bend) * (1.0 + (3 * gelu_cubic) * square)
        hidden_ref[:, at] = (active * up).astype(bf16)
        dup_ref[:, at] = (dhidden * active).astype(bf16)
        dgate_ref[:, at] = (dhidden * up * slope).astype(bf16)
    dnormed = (dot_nn(dgate_ref[...], gate_t[...]) + dot_nn(dup_ref[...], up_t[...])).astype(bf16)
    feed = dot_nn(hidden_ref[...], down[...]).astype(bf16)

    @pl.when(step < 2)
    def _():
        dnormed_keep[...] = dnormed
        feed_keep[...] = feed

    @pl.when(step >= 2)
    def _():
        sends[0] = dnormed
        sends[1] = feed


def feed_forward(order, row, normed_keep, normed_recv, grads, gate_t, up_t, down):
    units, width = down.shape
    length = 2 * normed_keep.shape[0]
    count = length // 4
    first = pl.BlockSpec((count, width), lambda step: (jnp.minimum(step, 1), 0))
    last = pl.BlockSpec((count, width), lambda step: (jnp.maximum(step - 2, 0), 0))
    pair = pl.BlockSpec((2, count, width), lambda step: (0, jnp.maximum(step - 2, 0), 0))
    each = pl.BlockSpec((count, units), lambda step: (step, 0))
    half = ((length // 2, width), bf16)
    return order.call(
        functools.partial(feed_kernel, 256),
        "feed_forward",
        (normed_keep, normed_recv, *grads, gate_t, up_t, down),
        [first, last, row_of(row, grads[0].shape), vmem, row_of(row, grads[2].shape), vmem] + [anywhere] * 3,
        [((length, units), bf16)] * 3 + [half, half, ((2, length // 2, width), bf16)],
        44,
        out_specs=[each] * 3 + [first, first, pair],
        grid=(4,),
        scratch=[pltpu.VMEM((units, width), bf16)] * 3 + [pltpu.SemaphoreType.DMA((3,))],
    )


def halves(parts, stride, bit):
    count, rows, width = parts.shape
    pairs = parts.reshape(count // (2 * stride), 2, stride, rows, width)
    low, high = pairs[:, 0], pairs[:, 1]
    shape = (count // 2, rows, width)
    return jnp.where(bit == 0, low, high).reshape(shape), jnp.where(bit == 0, high, low).reshape(shape)


def gradient_kernel(groups, bit, extra, place, *refs):
    rows = len(groups)
    extras, refs = refs[:extra], refs[extra:]
    lefts, refs = refs[: sum(map(len, groups))], refs[sum(map(len, groups)) :]
    rights_hbm, (kept_ref, sent_ref, left, right, left_sem, right_sem) = refs[:rows], refs[rows:]
    step, steps = pl.program_id(0), pl.num_programs(0)
    length, tile = left.shape[2], left.shape[3]

    def left_copies(row, at_step):
        taken = sum(map(len, groups[:row]))
        copies = []
        at = 0
        for index, lead in enumerate(groups[row]):
            source = lefts[taken + index]
            source = source if lead is None else source.at[lead]
            count = source.shape[0]
            cols = pl.ds(pl.multiple_of(at_step * tile, tile), tile)
            slot = lax.rem(at_step, 2)
            copies.append(
                pltpu.make_async_copy(
                    source.at[:, cols], left.at[slot, row, pl.ds(at, count)], left_sem.at[slot, taken + index]
                )
            )
            at += count
        return copies

    def right_copy(row):
        return pltpu.make_async_copy(rights_hbm[row], right.at[row], right_sem.at[row])

    @pl.when(step == 0)
    def _():
        for row in range(rows):
            for copy in left_copies(row, 0):
                copy.start()
            right_copy(row).start()

    @pl.when(step + 1 < steps)
    def _():
        for row in range(rows):
            for copy in left_copies(row, step + 1):
                copy.start()

    total = None
    for row in range(rows):
        for copy in left_copies(row, step):
            copy.wait()
        pl.when(step == 0)(right_copy(row).wait)
        part = dot_tn(left[lax.rem(step, 2), row], right[row])
        total = part if total is None else total + part
    if extra:
        added = sum(ref[0].astype(f32) for ref in extras)
        total = jnp.concatenate([total, added.T], axis=1)
    parts = total.reshape(-1, kept_ref.shape[1], kept_ref.shape[2])
    kept, sent = halves(parts, 1 << bit, place[2 + bit])
    kept_ref[...] = kept.astype(bf16)
    sent_ref[...] = sent.astype(bf16)


def gradient(order, name, place, lefts, rights, bit, extras=()):
    size = lax.axis_size("dp")
    length, cols = rights[0].shape
    width = lefts[0][0][0].shape[-1]
    tile = width // 2
    chunk_rows = width // size
    pieces = [piece for group in lefts for piece in group]
    rows = len(rights)
    all_cols = cols + (extras[0].shape[1] if extras else 0)
    return order.call(
        functools.partial(gradient_kernel, [[lead for _, lead in group] for group in lefts], bit, len(extras)),
        name,
        (place, *extras, *[array for array, _ in pieces], *rights),
        [smem]
        + [pl.BlockSpec((1, extra.shape[1], tile), lambda step: (0, 0, step)) for extra in extras]
        + [anywhere] * (len(pieces) + rows),
        [((size // 2, chunk_rows, all_cols), bf16)] * 2,
        40,
        out_specs=[pl.BlockSpec((size // 4, chunk_rows, all_cols), lambda step: (step, 0, 0))] * 2,
        grid=(2,),
        scratch=[
            pltpu.VMEM((2, rows, length, tile), bf16),
            pltpu.VMEM((rows, length, cols), bf16),
            pltpu.SemaphoreType.DMA((2, len(pieces))),
            pltpu.SemaphoreType.DMA((rows,)),
        ],
    )


def exchange(sent, bit):
    return lax.ppermute(sent, "dp", [(i, i ^ (1 << bit)) for i in range(lax.axis_size("dp"))])


def halve_kernel(stride, bit, place, kept, received, keep_ref, send_ref):
    parts = kept[...].astype(f32) + received[...].astype(f32)
    keep, send = halves(parts, stride, place[2 + bit])
    keep_ref[...] = keep.astype(bf16)
    send_ref[...] = send.astype(bf16)


class Scatter:
    def __init__(self, order, place, first, parts, finish):
        self.order, self.place, self.finish = order, place, finish
        count = lax.axis_size("dp").bit_length() - 1
        self.bits = list(range(first, count)) + list(range(first))
        self.left = sorted(self.bits)
        self.send(*parts)

    def send(self, kept, sent):
        bit = self.bits.pop(0)
        self.left.remove(bit)
        self.parts = kept, exchange(sent, bit)

    def step(self):
        kept, received = self.parts
        if not self.bits:
            return self.finish(self.order, kept, received)
        bit = self.bits[0]
        stride = 1 << self.left.index(bit)
        shape = (kept.shape[0] // 2,) + kept.shape[1:]
        self.send(
            *self.order.call(
                functools.partial(halve_kernel, stride, bit),
                "halve",
                (self.place, kept, received),
                [smem] + [vmem] * 2,
                [(shape, bf16)] * 2,
                12,
            )
        )

    def run(self):
        result = None
        while result is None:
            result = self.step()
        return result


def joined_kernel(kept, received, out):
    out[...] = kept[0].astype(f32) + received[0].astype(f32)


def finish_joined(order, kept, received):
    return order.call(joined_kernel, "gradient_output", (kept, received), [vmem] * 2, [(kept.shape[1:], f32)], 8)[0]


def projections_kernel(kept, received, query, key, value, out):
    total = kept[0].astype(f32) + received[0].astype(f32)
    cols = total.shape[1] // 4
    for index, target in enumerate((query, key, value)):
        target[...] = total[:, index * cols : (index + 1) * cols]
    out[...] = total[:, 3 * cols :].T


def finish_projections(order, kept, received):
    rows, cols = kept.shape[1], kept.shape[2] // 4
    return order.call(
        projections_kernel,
        "projection_outputs",
        (kept, received),
        [vmem] * 2,
        [((rows, cols), f32)] * 3 + [((cols, rows), f32)],
        8,
    )


def pass_kernel(*refs):
    for keep, received, out in zip(refs[0::2], refs[1::2], refs[-(len(refs) // 3) :]):
        out[...] = (keep[...].reshape(out.shape).astype(f32) + received[...].reshape(out.shape).astype(f32)).astype(bf16)


def pass_on(order, keep, received, lead=None):
    count, width = keep.shape[0] // 2, keep.shape[1]
    second = pl.BlockSpec((count, width), lambda *_: (1, 0))
    other = second if lead is None else pl.BlockSpec((1, count, width), lambda *_: (lead, 1, 0))
    return over_y(
        order.call(pass_kernel, "pass_on", (keep, received), [second, other], [((count, width), bf16)], 8)[0]
    )


def pass_rows_kernel(*refs):
    out = refs[-1]
    for row in range(out.shape[0]):
        out[row] = (refs[2 * row][...].astype(f32) + refs[2 * row + 1][0].astype(f32)).astype(bf16)


def pass_rows(order, parts, lead):
    count, width = parts[0][0].shape[0] // 2, parts[0][0].shape[1]
    second = pl.BlockSpec((count, width), lambda *_: (1, 0))
    other = pl.BlockSpec((1, count, width), lambda *_: (lead, 1, 0))
    return over_y(
        order.call(
            pass_rows_kernel,
            "pass_on",
            [array for pair in parts for array in pair],
            [second, other] * len(parts),
            [((len(parts), count, width), bf16)],
            12,
        )[0]
    )


def outproj_pass(order, keep, received):
    shape = keep.shape[1:]
    second = pl.BlockSpec((1,) + shape, lambda *_: (1, 0, 0))
    return over_y(order.call(pass_kernel, "pass_on", (keep, received), [second] * 2, [((1,) + shape, bf16)], 8)[0])


def relay_kernel(source, target):
    target[...] = source[0] if len(source.shape) == 3 else source[...]


def relay(order, array, row=None):
    shape = array.shape if row is None else array.shape[1:]
    spec = vmem if row is None else row_of(row, array.shape)
    return order.call(relay_kernel, "relay", (array,), [spec], [(shape, array.dtype)], 8)[0]


def summed(keep, received, from_y):
    shape = keep.shape
    return sum(ref[...].reshape(shape).astype(f32) for ref in (keep, received, from_y))


def block_out_kernel(middle, keep, received, from_y, _, out):
    out[0] = middle[...] + summed(keep, received, from_y)


def input_grad_kernel(dmiddle, keep, received, from_y, inputs, gain, _, out):
    dnormed = summed(keep, received, from_y)
    out[0] = dmiddle[...] + norm_backward(dnormed, inputs[0].astype(f32), gain[...])


def place_row(order, kernel, name, row, before, summed, inputs, in_specs, lead=None):
    keep, received, from_y = summed
    count, width = from_y.shape[-2:]
    first = pl.BlockSpec((count, width), lambda *_: (0, 0))
    pair = first if len(received.shape) == 2 else pl.BlockSpec((1, count, width), lambda *_: (lead, 0, 0))
    arrived = vmem if len(from_y.shape) == 2 else row_of(row, from_y.shape)
    specs = [vmem, first, pair, arrived] + in_specs + [anywhere]
    return order.call(
        kernel,
        name,
        (inputs[0], keep, received, from_y, *inputs[1:], before),
        specs,
        [(before.shape, f32)],
        16,
        out_specs=[row_of(row, before.shape)],
        aliases={len(specs) - 1: 0},
    )[0]


def add_kernel(*refs):
    refs[-1][...] = sum(ref[...] for ref in refs[:-1])


def add_all(order, arrays):
    return order.call(add_kernel, "small_sum", arrays, [vmem] * len(arrays), [(arrays[0].shape, f32)], 4)[0]


def small_rounds(order, vector):
    count = lax.axis_size("dp").bit_length() - 1
    moved = [over_core(vector), over_y(vector), over_both(vector)]
    yield None
    vector = add_all(order, [vector, *moved])
    for low in range(0, count, 2):
        masks = [mask << low for mask in (1, 2, 3) if mask << low < 1 << count]
        moved = [lax.ppermute(vector, "dp", [(i, i ^ mask) for i in range(1 << count)]) for mask in masks]
        yield None
        vector = add_all(order, [vector, *moved])
    yield vector


def per_device(
    block_input,
    out_grad,
    seg_lengths,
    norm1_gain,
    norm2_gain,
    rel_bias,
    w_query,
    w_key,
    w_value,
    w_out,
    w_gate,
    w_up,
    w_down,
):
    rows, count, width = block_input.shape
    length = 4 * count
    here = lax.axis_index("tensor")
    dp_bits = lax.axis_size("dp").bit_length() - 1
    dp_at = lax.axis_index("dp")
    place = jnp.stack([here // 2, here % 2] + [(dp_at >> bit) & 1 for bit in range(dp_bits)]).astype(jnp.int32)
    head_width = w_query.shape[1]
    heads = head_width // DK
    buckets = rel_bias.shape[0]
    gain_one = norm1_gain.astype(f32)[None]
    gain_two = norm2_gain.astype(f32)[None]
    first_head = here * heads
    weight_t = jnp.concatenate([w_query.T, w_key.T, w_value.T], axis=0)
    gate_t, up_t = w_gate.T, w_up.T

    order = Order()
    every_row = range(rows)
    last_row = rows - 1

    band, far = bias_parts(lax.dynamic_slice_in_dim(rel_bias, first_head, heads, 1), length)
    order.after(band, far, weight_t)
    input_y = [over_y(block_input[0])]
    input_core = over_core(block_input)
    grad_core = over_core(out_grad)
    out_core = over_core(w_out)
    order.after(grad_core, out_core)
    for row in range(1, rows):
        order.after(input_y[-1])
        input_y.append(over_y(relay(order, block_input, row)))

    normed_one, qkvs, logsums, attended, middles = [], [], [], [], []
    grad_y, grad_both = [], []
    normed_keeps, normed_recvs = [], []

    def second_norm(row):
        middle, normed_keep = attention_branch(
            order, row, attended[row], out_parts, block_input, input_y[row], gain_two
        )
        middles.append(middle)
        normed_keeps.append(normed_keep)
        normed_recvs.append(over_core(normed_keep))

    for row in every_row:
        normed, qkv = project(
            order, row, (block_input, input_y[row], input_core, over_core(input_y[row])), gain_one, weight_t
        )
        if row == 0:
            out_y = over_y(relay(order, w_out))
        keep, send, logsum = attention_forward(order, row, place, seg_lengths, qkv, band, far)
        other = over_core(send)
        normed_one.append(normed)
        qkvs.append(qkv)
        logsums.append(logsum)
        attended.append([keep, other, over_y(keep), over_y(other)])
        if row == 0:
            order.after(out_y)
            out_both = over_core(out_y)
            out_parts = [w_out, out_core, out_y, out_both]
        else:
            second_norm(row - 1)
        if row < last_row:
            order.after(input_y[row + 1])
        order.after(other)
        if grad_y:
            order.after(grad_y[-1])
        grad_y.append(over_y(relay(order, out_grad, row)))
        if row > 0:
            grad_both.append(over_core(grad_y[row - 1]))

    hiddens, dgates, dups, dnormed, feeds = [], [], [], [], []

    def feed(row):
        hidden, dgate, dup, dn_keep, ff_keep, sends = feed_forward(
            order,
            row,
            normed_keeps[row],
            normed_recvs[row],
            (out_grad, grad_y[row], grad_core, grad_both[row]),
            gate_t,
            up_t,
            w_down,
        )
        hiddens.append(hidden)
        dgates.append(dgate)
        dups.append(dup)
        received = over_core(sends)
        dnormed.append([dn_keep, received])
        feeds.append([ff_keep, received])

    feed(0)
    second_norm(last_row)
    grad_both.append(over_core(relay(order, grad_y[last_row])))
    dnormed[0].append(pass_on(order, *dnormed[0], lead=0))
    for row in range(1, rows):
        feed(row)
    grad_pieces = [[(out_grad, r), (grad_y[r], None), (grad_core, r), (grad_both[r], None)] for r in every_row]
    normed_pieces = [[(normed_keeps[r], None), (normed_recvs[r], None)] for r in every_row]
    down_scatter = Scatter(
        order, place, 0, gradient(order, "down_gradient", place, grad_pieces, hiddens, 0), finish_joined
    )
    for row in range(1, rows):
        dnormed[row].append(pass_on(order, *dnormed[row], lead=0))

    band_grad = jnp.zeros(band.shape, f32)
    far_grad = jnp.zeros((8, 2 * LANES), f32)
    dmiddles, dbranches, dqkvs, norm1_sums, norm2_sums, inner = [], [], [], [], [], []
    for row in every_row:
        if row > 0:
            order.after(feeds_y)
        dmiddle, dbranch, norm2_sum, dout_own, dout_core, dout_y = branch_backward(
            order, row, *dnormed[row], middles[row], out_grad, gain_two, out_parts
        )
        dmiddles.append(dmiddle)
        dbranches.append(dbranch)
        norm2_sums.append(norm2_sum)
        dout_y = over_y(dout_y)
        if row == 0:
            gate_scatter = Scatter(
                order, place, 1, gradient(order, "gate_gradient", place, normed_pieces, dgates, 1), finish_joined
            )
        else:
            down_scatter.step()
            gate_scatter.step()
        order.after(dout_y)
        dout_core = over_core(jnp.stack([dout_core, dout_y[1]]))
        if row == 0:
            up_scatter = Scatter(
                order, place, 0, gradient(order, "up_gradient", place, normed_pieces, dups, 0), finish_joined
            )
            down_scatter.step()
            feeds_y = pass_rows(order, feeds, 1)
        else:
            inner[0].append(pass_on(order, *inner[0]))
            out_keep, out_send = outproj_grad(order, [part for group in attended for part in group], dbranches)
            out_recv = over_core(out_send)
        dqkv, dn_keep, dn_send, band_grad, far_grad, norm1_sum = attention_backward(
            order, row, place, seg_lengths, qkvs[row], (dout_own, dout_y, dout_core), logsums[row], band, far,
            weight_t, normed_one[row], band_grad, far_grad,
        )
        norm1_sums.append(norm1_sum)
        dqkvs.append(dqkv)
        inner.append([dn_keep, over_core(dn_send)])
    out_from_y = outproj_pass(order, out_keep, out_recv)
    up_scatter.step()
    for row in range(1, rows):
        inner[row].append(pass_on(order, *inner[row]))
    qkv_scatter = Scatter(
        order,
        place,
        0,
        gradient(
            order,
            "projection_gradient",
            place,
            [[(normed_one[r], None)] for r in every_row],
            dqkvs,
            0,
            (out_keep, out_recv, out_from_y),
        ),
        finish_projections,
    )
    down_out = down_scatter.run()
    block_out = jnp.zeros((rows, count, width), f32)
    input_grad = jnp.zeros((rows, count, width), f32)
    for row in every_row:
        block_out = place_row(
            order, block_out_kernel, "block_output", row, block_out, (*feeds[row], feeds_y), (middles[row],), [], 1
        )
    gate_out = gate_scatter.run()
    up_scatter.step()

    norm1_sum = sum(norm1_sums)[0] / gain_one[0]
    norm2_sum = sum(norm2_sums)[0]
    index = band_buckets(buckets)
    bucket_sum = jnp.einsum(
        "bkp,hkp->bh",
        (index[None] == jnp.arange(buckets, dtype=jnp.int32)[:, None, None]).astype(bf16),
        band_grad.astype(bf16),
        preferred_element_type=f32,
    )
    far_sums = jnp.sum(far_grad[:heads].reshape(heads, 2, LANES), axis=2)
    bucket_sum = bucket_sum.at[buckets // 2 - 1].add(far_sums[:, 0]).at[buckets - 1].add(far_sums[:, 1])
    bias_sum = lax.dynamic_update_slice(jnp.zeros(rel_bias.shape, f32), bucket_sum, (0, first_head))
    small = jnp.concatenate([norm1_sum, norm2_sum, bias_sum.reshape(-1)])[None]
    small = relay(order, small)
    rounds = small_rounds(order, small)
    small = next(rounds)
    qkv_scatter.step()
    small = next(rounds)
    for row in range(rows):
        input_grad = place_row(
            order,
            input_grad_kernel,
            "input_gradient",
            row,
            input_grad,
            inner[row],
            (dmiddles[row], block_input, gain_one),
            [row_of(row, block_input.shape), vmem],
        )
    up_out = up_scatter.run()
    qkv_scatter.step()
    while small is None:
        small = next(rounds)
    small = small[0]
    query_out, key_out, value_out, outproj_out = qkv_scatter.run()

    return (
        block_out,
        input_grad,
        small[:width],
        small[width : 2 * width],
        small[2 * width :].reshape(rel_bias.shape),
        query_out,
        key_out,
        value_out,
        outproj_out,
        gate_out,
        up_out,
        down_out.T,
    )


def solution(mesh):
    in_specs = (
        P("dp", "tensor", None),
        P("dp", "tensor", None),
        P("dp", None),
        P(),
        P(),
        P(),
        P(None, "tensor"),
        P(None, "tensor"),
        P(None, "tensor"),
        P("tensor", None),
        P(None, "tensor"),
        P(None, "tensor"),
        P("tensor", None),
    )
    out_specs = (
        P("dp", "tensor", None),
        P("dp", "tensor", None),
        P(),
        P(),
        P(),
        P("dp", "tensor"),
        P("dp", "tensor"),
        P("dp", "tensor"),
        P("tensor", "dp"),
        P("dp", "tensor"),
        P("dp", "tensor"),
        P("tensor", "dp"),
    )
    return jax.shard_map(
        per_device, mesh=mesh, in_specs=in_specs, out_specs=out_specs, check_vma=False
    )
```

time: 1430 us -> 465 us (0.33)
  waiting for transfers between devices: 904 us -> 94.3 us
  matrix products: 376 us -> 3.95 us
  Pallas kernels: 0 us -> 262 us
  other arithmetic: 65 us -> 19.5 us
  starting transfers between devices: 0.62 us -> 46 us
  blocking collectives: 41.2 us -> 0 us
  local copies, waits for them, and re-layouts: 14 us -> 33.3 us
    reduce_scatter x10 -> x0, waiting for transfers between devices: 764 us -> none  [the longest x1 121 us: per_device(): lax.psum_scatter(up_grad, 'dp', scatter_dimension=0, tiled=True)]
    dot_general x51 -> x1, matrix products: 376 us -> 3.95 us  [per_device(): jnp.einsum('bkp,hkp->bh', (index[None] == jnp.arange(buckets, dtype=jnp.i...]
    pallas_call x0 -> x48, Pallas kernels: none -> 262 us  [call(): pl.pallas_call(body, grid=grid, in_specs=list(in_specs) + [anywhere] * ex...]
    all_gather x4 -> x0, waiting for transfers between devices: 138 us -> none  [the longest x1 46.5 us: per_device(): full_branch = lax.all_gather(dbranch, 'tensor', axis=1, tiled=True)]
    ppermute x0 -> x55, waiting for transfers between devices: none -> 94.3 us  [the longest x12 48.3 us: exchange(): lax.ppermute(sent, 'dp', [(i, i ^ 1 << bit) for i in range(lax.axis_size(...]
    ppermute x0 -> x55, starting transfers between devices: none -> 46 us  [the longest x18 19.6 us: over_y(): return lax.ppermute(array, 'tensor', across_y)]
    psum x1 -> x0, blocking collectives: 41.2 us -> none  [per_device(): lax.psum((gain_one_grad, gain_two_grad, bias_full), ('dp', 'tensor'))]
    sub x4 -> x1, other arithmetic: 17.5 us -> 0.01 us  [band_buckets(): key = jnp.arange(QUERY_BLOCK + 2 * REACH, dtype=jnp.int32) - REACH]
  transfers between devices with their start and end apart: 15 -> 55, of which waited for: 13 -> 15; matrix products, arithmetic and copies ran while one was open for 17% -> 8% of each run, Pallas kernels for 0% -> 56%
where the time goes in v1:
time: 465 us; the launch traced here: 461 us
  Pallas kernels  262 us (56%)
  waiting for transfers between devices  94.3 us (20%)
  starting transfers between devices  46 us (10%)
  local copies, waits for them, and re-layouts  33.3 us (7%)
  other arithmetic  19.5 us (4%)
    pallas_call x48, Pallas kernels, call(): pl.pallas_call(body, grid=grid, in_specs=list(in_specs) + [anywhere] * ex...  262 us
    ppermute x12, waiting for transfers between devices, exchange(): lax.ppermute(sent, 'dp', [(i, i ^ 1 << bit) for i in range(lax.axis_size(...  48.3 us
    ppermute x18, waiting for transfers between devices, over_y(): return lax.ppermute(array, 'tensor', across_y)  40.7 us
    unnamed x205, local copies, waits for them, and re-layouts  24.7 us
    ppermute x18, starting transfers between devices, over_y(): return lax.ppermute(array, 'tensor', across_y)  19.6 us
    ppermute x12, starting transfers between devices, exchange(): lax.ppermute(sent, 'dp', [(i, i ^ 1 << bit) for i in range(lax.axis_size(...  17.6 us
  transfers between devices with their start and end apart: 55, of which 15 were waited for; matrix products, arithmetic and copies ran while one was open for 8% of the time, Pallas kernels for 56%

profile of v1, /device:TPU:0, one launch (start us, length us, event | category | flops | bytes accessed | tf_op | source)
XLA Modules:
  0.0 460.7 jit_solution(17669683213533317148)
XLA Ops:
  12.1 5.2 %select_select_fusion.refs_1_.refs_3_.refs_7_ = f32[3,512,256]{2,1,0:T(8,128)S(1)} fusion(f32[3]{0:T(128)S(1)} %get-tuple-element.247, f32[3]{0:T(128)S(1)} %get-tuple-element.248, f32[3]{0:T(128)S(1)} %get-tuple-element.249, f32[3]{0:T(128)S(1)} %get-tuple-element.250, f32[3]{0:T(128)S(1)} %get-tuple-element.251, f32[3]{0:T(128)S(1)} %get-tuple-element.252, ...), kind=kLoop, calls=%fused_computation.4 | loop fusion | flops 12582912 | bytes 5767552 | tf_op jit(solution)/shard_map/jit(_where)/select_n | solution.py:145
  28.1 4.8 %normed_projections.2 = (bf16[1024,1536]{1,0:T(8,128)(2,1)S(1)}, bf16[1024,576]{1,0:T(8,128)(2,1)S(1)}) custom-call(bf16[2,256,1536]{2,1,0:T(8,128)(2,1)S(1)} %copy-done.9, bf16[256,1536]{1,0:T(8,128)(2,1)} %collective-permute-done.2.refs_6_.refs_1_.refs_9_, bf16[2,256,1536]{2,1,0:T(8,128)(2,1)} %collective-permute-done.4.refs_2_, ...), custom_call_target="tpu_custom_call" | custom-call | flops 9999999827968 | bytes 1024 | tf_op jit(solution)/shard_map/normed_projections/pallas_call | solution.py:76
  35.8 12.2 %attention_forward.2 = (bf16[512,192]{1,0:T(8,128)(2,1)}, bf16[512,192]{1,0:T(8,128)(2,1)S(1)}, f32[8,1024]{1,0:T(8,128)S(1)}) custom-call(s32[5]{0:T(128)S(1)} %stack.35.refs_0_, s32[2,4]{1,0:T(2,128)S(1)} %copy-done.22, bf16[1024,576]{1,0:T(8,128)(2,1)S(1)} %get-tuple-element.116.refs_2_, f32[3,512,256]{2,1,0:T(8,128)S(1)} %select_select_fusion.refs_1_.refs_3_.refs_7_, ...), custom_call_target="tpu_custom_call" | custom-call | flops 9999999827968 | bytes 1024 | tf_op jit(solution)/shard_map/attention_forward/pallas_call | solution.py:76
  51.5 8.1 %collective-permute-done.7.refs_2_.refs_6_.refs_8_ = bf16[192,1536]{1,0:T(8,128)(2,1)} collective-permute-done((bf16[192,1536]{1,0:T(8,128)(2,1)}, bf16[192,1536]{1,0:T(8,128)(2,1)}, u32[]{:S(2)}, u32[]{:S(2)}) %collective-permute-start.7) | collective-permute-done | bytes 589856 | tf_op jit(solution)/shard_map/ppermute | solution.py:43
  63.0 4.8 %normed_projections.3 = (bf16[1024,1536]{1,0:T(8,128)(2,1)S(1)}, bf16[1024,576]{1,0:T(8,128)(2,1)S(1)}) custom-call(bf16[2,256,1536]{2,1,0:T(8,128)(2,1)S(1)} %copy-done.10, bf16[256,1536]{1,0:T(8,128)(2,1)} %collective-permute-done.3.refs_3_.refs_1_.refs_9_, bf16[2,256,1536]{2,1,0:T(8,128)(2,1)} %collective-permute-done.4.refs_2_, ...), custom_call_target="tpu_custom_call" | custom-call | flops 9999999827968 | bytes 1024 | tf_op jit(solution)/shard_map/normed_projections/pallas_call | solution.py:76
  67.9 12.5 %attention_forward.3 = (bf16[512,192]{1,0:T(8,128)(2,1)}, bf16[512,192]{1,0:T(8,128)(2,1)}, f32[8,1024]{1,0:T(8,128)S(1)}) custom-call(s32[5]{0:T(128)S(1)} %stack.35.refs_0_, s32[2,4]{1,0:T(2,128)S(1)} %copy-done.23, bf16[1024,576]{1,0:T(8,128)(2,1)S(1)} %get-tuple-element.120.refs_2_, f32[3,512,256]{2,1,0:T(8,128)S(1)} %select_select_fusion.refs_1_.refs_3_.refs_7_, ...), custom_call_target="tpu_custom_call" | custom-call | flops 9999999827968 | bytes 1024 | tf_op jit(solution)/shard_map/attention_forward/pallas_call | solution.py:76
  82.4 5.3 %attention_branch.2 = (f32[256,1536]{1,0:T(8,128)S(1)}, bf16[512,1536]{1,0:T(8,128)(2,1)}) custom-call(bf16[512,192]{1,0:T(8,128)(2,1)} %get-tuple-element.118.refs_1_.refs_0_, bf16[512,192]{1,0:T(8,128)(2,1)} %collective-permute-done.8.refs_4_.refs_1_, bf16[512,192]{1,0:T(8,128)(2,1)} %collective-permute-done.13.refs_2_, ...), custom_call_target="tpu_custom_call" | custom-call | flops 9999999827968 | bytes 1024 | tf_op jit(solution)/shard_map/attention_branch/pallas_call | solution.py:76
  92.6 29.8 %feed_forward.2 = (bf16[1024,992]{1,0:T(8,128)(2,1)}, bf16[1024,992]{1,0:T(8,128)(2,1)}, bf16[1024,992]{1,0:T(8,128)(2,1)}, bf16[512,1536]{1,0:T(8,128)(2,1)S(1)...) custom-call(bf16[512,1536]{1,0:T(8,128)(2,1)} %get-tuple-element.124.refs_0_.refs_1_, ...), custom_call_target="tpu_custom_call" | custom-call | flops 9999999827968 | bytes 1024 | tf_op jit(solution)/shard_map/feed_forward/pallas_call | solution.py:76
  125.2 5.2 %attention_branch.3 = (f32[256,1536]{1,0:T(8,128)S(1)}, bf16[512,1536]{1,0:T(8,128)(2,1)}) custom-call(bf16[512,192]{1,0:T(8,128)(2,1)} %get-tuple-element.122.refs_11_.refs_0_.refs_4_, bf16[512,192]{1,0:T(8,128)(2,1)} %collective-permute-done.9.refs_2_.refs_1_.refs_5_, bf16[512,192]{1,0:T(8,128)(2,1)} %collective-permute-done.10.refs_2_.refs_6_, ...), custom_call_target="tpu_custom_call" | custom-call | flops 9999999827968 | bytes 1024 | tf_op jit(solution)/shard_map/attention_branch/pallas_call | solution.py:76
  138.0 30.0 %feed_forward.3 = (bf16[1024,992]{1,0:T(8,128)(2,1)}, bf16[1024,992]{1,0:T(8,128)(2,1)}, bf16[1024,992]{1,0:T(8,128)(2,1)}, bf16[512,1536]{1,0:T(8,128)(2,1)S(1)...) custom-call(bf16[512,1536]{1,0:T(8,128)(2,1)} %get-tuple-element.128.refs_0_.refs_3_, ...), custom_call_target="tpu_custom_call" | custom-call | flops 9999999827968 | bytes 1024 | tf_op jit(solution)/shard_map/feed_forward/pallas_call | solution.py:76
  170.8 10.4 %down_gradient.1 = (bf16[4,192,992]{2,1,0:T(8,128)(2,1)S(1)}, bf16[4,192,992]{2,1,0:T(8,128)(2,1)}) custom-call(s32[5]{0:T(128)S(1)} %stack.35.refs_0_, bf16[2,256,1536]{2,1,0:T(8,128)(2,1)S(1)} %copy-done.15, bf16[256,1536]{1,0:T(8,128)(2,1)} %collective-permute-done.16.refs_3_.refs_2_, bf16[2,256,1536]{2,1,0:T(8,128)(2,1)S(1)} %copy-done.17, ...), custom_call_target="tpu_custom_call" | custom-call | flops 9999999827968 | bytes 1024 | tf_op jit(solution)/shard_map/down_gradient/pallas_call | solution.py:76
  192.1 11.4 %gate_gradient.1 = (bf16[4,192,992]{2,1,0:T(8,128)(2,1)S(1)}, bf16[4,192,992]{2,1,0:T(8,128)(2,1)}) custom-call(s32[5]{0:T(128)S(1)} %stack.35.refs_0_, bf16[512,1536]{1,0:T(8,128)(2,1)} %get-tuple-element.124.refs_0_.refs_1_, bf16[512,1536]{1,0:T(8,128)(2,1)} %collective-permute-done.15.refs_1_.refs_2_, ...), custom_call_target="tpu_custom_call" | custom-call | flops 9999999827968 | bytes 1024 | tf_op jit(solution)/shard_map/gate_gradient/pallas_call | solution.py:76
  205.2 5.6 %collective-permute-done.25.refs_8_.refs_4_ = bf16[2,256,192]{2,1,0:T(8,128)(2,1)} collective-permute-done((bf16[2,256,192]{2,1,0:T(8,128)(2,1)}, bf16[2,256,192]{2,1,0:T(8,128)(2,1)}, u32[]{:S(2)}, u32[]{:S(2)}) %collective-permute-start.25) | collective-permute-done | bytes 196640 | tf_op jit(solution)/shard_map/ppermute | solution.py:43
  212.4 11.7 %up_gradient.1 = (bf16[4,192,992]{2,1,0:T(8,128)(2,1)S(1)}, bf16[4,192,992]{2,1,0:T(8,128)(2,1)}) custom-call(s32[5]{0:T(128)S(1)} %stack.35.refs_0_, bf16[512,1536]{1,0:T(8,128)(2,1)} %get-tuple-element.124.refs_0_.refs_1_, bf16[512,1536]{1,0:T(8,128)(2,1)} %collective-permute-done.15.refs_1_.refs_2_, bf16[512,1536]{1,0:T(8,128)(2,1)} %get-tuple-element.128.refs_0_.refs_3_, ...), custom_call_target="tpu_custom_call" | custom-call | flops 9999999827968 | bytes 1024 | tf_op jit(solution)/shard_map/up_gradient/pallas_call | solution.py:76
  236.2 19.2 %attention_backward.2 = (bf16[1024,576]{1,0:T(8,128)(2,1)S(1)}, bf16[512,1536]{1,0:T(8,128)(2,1)S(1)}, bf16[512,1536]{1,0:T(8,128)(2,1)}, f32[3,512,256]{2,1,0:T...) custom-call(s32[5]{0:T(128)S(1)} %stack.35.refs_0_, s32[2,4]{1,0:T(2,128)S(1)} %copy-done.24, ...), custom_call_target="tpu_custom_call" | custom-call | flops 9999999827968 | bytes 1024 | tf_op jit(solution)/shard_map/attention_backward/pallas_call | solution.py:76
  255.4 12.5 %collective-permute-done.26.refs_11_.refs_3_ = bf16[2,256,1536]{2,1,0:T(8,128)(2,1)} collective-permute-done((bf16[2,256,1536]{2,1,0:T(8,128)(2,1)}, bf16[2,256,1536]{2,1,0:T(8,128)(2,1)}, u32[]{:S(2)}, u32[]{:S(2)}) %collective-permute-start.26) | collective-permute-done | bytes 1572896 | tf_op jit(solution)/shard_map/ppermute | solution.py:43
  291.3 19.9 %attention_backward.3 = (bf16[1024,576]{1,0:T(8,128)(2,1)S(1)}, bf16[512,1536]{1,0:T(8,128)(2,1)}, bf16[512,1536]{1,0:T(8,128)(2,1)}, f32[3,512,256]{2,1,0:T(8,1...) custom-call(s32[5]{0:T(128)S(1)} %stack.35.refs_0_, s32[2,4]{1,0:T(2,128)S(1)} %copy-done.25, ...), custom_call_target="tpu_custom_call" | custom-call | flops 9999999827968 | bytes 1024 | tf_op jit(solution)/shard_map/attention_backward/pallas_call | solution.py:76
  328.9 9.8 %collective-permute-done.36.refs_3_ = bf16[1,192,1536]{2,1,0:T(8,128)(2,1)} collective-permute-done((bf16[1,192,1536]{2,1,0:T(8,128)(2,1)}, bf16[1,192,1536]{2,1,0:T(8,128)(2,1)}, u32[]{:S(2)}, u32[]{:S(2)}) %collective-permute-start.36) | collective-permute-done | bytes 589856 | tf_op jit(solution)/shard_map/ppermute | solution.py:43
  338.7 9.4 %projection_gradient.1 = (bf16[4,192,768]{2,1,0:T(8,128)(2,1)S(1)}, bf16[4,192,768]{2,1,0:T(8,128)(2,1)}) custom-call(s32[5]{0:T(128)S(1)} %stack.35.refs_0_, bf16[2,192,1536]{2,1,0:T(8,128)(2,1)S(1)} %copy-done.76, bf16[2,192,1536]{2,1,0:T(8,128)(2,1)} %collective-permute-done.34.refs_1_.refs_2_, bf16[1,192,1536]{2,1,0:T(8,128)(2,1)} %collective-permute-done.36.refs_3_, ...), custom_call_target="tpu_custom_call" | custom-call | flops 9999999827968 | bytes 1024 | tf_op jit(solution)/shard_map/projection_gradient/pallas_call | solution.py:76
  369.0 7.1 %collective-permute-done.43.refs_1_ = bf16[1,192,992]{2,1,0:T(8,128)(2,1)S(1)} collective-permute-done((bf16[1,192,992]{2,1,0:T(8,128)(2,1)S(1)}, bf16[1,192,992]{2,1,0:T(8,128)(2,1)S(1)}, u32[]{:S(2)}, u32[]{:S(2)}) %collective-permute-start.43) | collective-permute-done | bytes 380960 | tf_op jit(solution)/shard_map/ppermute | solution.py:601
  377.1 7.4 %collective-permute-done.41.refs_2_ = bf16[2,192,992]{2,1,0:T(8,128)(2,1)} collective-permute-done((bf16[2,192,992]{2,1,0:T(8,128)(2,1)}, bf16[2,192,992]{2,1,0:T(8,128)(2,1)}, u32[]{:S(2)}, u32[]{:S(2)}) %collective-permute-start.41) | collective-permute-done | bytes 761888 | tf_op jit(solution)/shard_map/ppermute | solution.py:601
  389.1 10.9 %collective-permute-done.47.refs_2_ = bf16[4,192,768]{2,1,0:T(8,128)(2,1)} collective-permute-done((bf16[4,192,768]{2,1,0:T(8,128)(2,1)}, bf16[4,192,768]{2,1,0:T(8,128)(2,1)}, u32[]{:S(2)}, u32[]{:S(2)}) %collective-permute-start.47) | collective-permute-done | bytes 1179680 | tf_op jit(solution)/shard_map/ppermute | solution.py:601
  427.8 8.6 %collective-permute-done.51.refs_2_ = bf16[2,192,768]{2,1,0:T(8,128)(2,1)} collective-permute-done((bf16[2,192,768]{2,1,0:T(8,128)(2,1)}, bf16[2,192,768]{2,1,0:T(8,128)(2,1)}, u32[]{:S(2)}, u32[]{:S(2)}) %collective-permute-start.51) | collective-permute-done | bytes 589856 | tf_op jit(solution)/shard_map/ppermute | solution.py:601
  446.6 11.8 %collective-permute-done.54.refs_1_ = bf16[1,192,768]{2,1,0:T(8,128)(2,1)} collective-permute-done((bf16[1,192,768]{2,1,0:T(8,128)(2,1)}, bf16[1,192,768]{2,1,0:T(8,128)(2,1)}, u32[]{:S(2)}, u32[]{:S(2)}) %collective-permute-start.54) | collective-permute-done | bytes 294944 | tf_op jit(solution)/shard_map/ppermute | solution.py:601
  (385 shorter events, 185.0 us)
Async XLA Ops:
  26.3 33.3 %collective-permute-start.3 = (bf16[256,1536]{1,0:T(8,128)(2,1)}, bf16[256,1536]{1,0:T(8,128)(2,1)}, u32[]{:S(2)}, u32[]{:S(2)}) collective-permute-start(bf16[256,1536]{1,0:T(8,128)(2,1)} %relay.6.refs_6_), channel_id=1, source_target_pairs={{0,2},{2,0},{1,3},{3,1},{4,6},{6,4},{5,7},{7,5},{8,10},{10,8},{9,1... | collective-permute-start | bytes 2359304 | tf_op jit(solution)/shard_map/ppermute | solution.py:43
  49.4 31.2 %collective-permute-start.13 = (bf16[512,192]{1,0:T(8,128)(2,1)}, bf16[512,192]{1,0:T(8,128)(2,1)}, u32[]{:S(2)}, u32[]{:S(2)}) collective-permute-start(bf16[512,192]{1,0:T(8,128)(2,1)} %get-tuple-element.118.refs_1_.refs_0_), channel_id=1, source_target_pairs={{0,2},{2,0},{1,3},{3,1},{4,6},{6,4},{5,7},{7,5},{8,10},{10,8},{9,1... | collective-permute-start | bytes 589832 | tf_op jit(solution)/shard_map/ppermute | solution.py:43
  50.3 32.0 %collective-permute-start.14 = (bf16[512,192]{1,0:T(8,128)(2,1)}, bf16[512,192]{1,0:T(8,128)(2,1)}, u32[]{:S(2)}, u32[]{:S(2)}) collective-permute-start(bf16[512,192]{1,0:T(8,128)(2,1)} %collective-permute-done.8.refs_4_.refs_1_), channel_id=1, source_target_pairs={{0,2},{2,0},{1,3},{3,1},{4,6},{6,4},{5,7},{7,5},{8,10},{10,8},{9,1... | collective-permute-start | bytes 589832 | tf_op jit(solution)/shard_map/ppermute | solution.py:43
  61.0 26.8 %collective-permute-start.16 = (bf16[256,1536]{1,0:T(8,128)(2,1)}, bf16[256,1536]{1,0:T(8,128)(2,1)}, u32[]{:S(2)}, u32[]{:S(2)}) collective-permute-start(bf16[256,1536]{1,0:T(8,128)(2,1)} %relay.8.refs_6_), channel_id=1, source_target_pairs={{0,2},{2,0},{1,3},{3,1},{4,6},{6,4},{5,7},{7,5},{8,10},{10,8},{9,1... | collective-permute-start | bytes 2359304 | tf_op jit(solution)/shard_map/ppermute | solution.py:43
  80.6 42.1 %collective-permute-start.10 = (bf16[512,192]{1,0:T(8,128)(2,1)}, bf16[512,192]{1,0:T(8,128)(2,1)}, u32[]{:S(2)}, u32[]{:S(2)}) collective-permute-start(bf16[512,192]{1,0:T(8,128)(2,1)} %get-tuple-element.122.refs_11_.refs_0_.refs_4_), channel_id=1, source_target_pairs={{0,2},{2,0},{1,3},{3,1},{4,6},{6,4},{5,7},{7,5},{8,10},{10,8},{9,1... | collective-permute-start | bytes 589832 | tf_op jit(solution)/shard_map/ppermute | solution.py:43
  89.2 41.2 %collective-permute-start.19 = (bf16[256,1536]{1,0:T(8,128)(2,1)}, bf16[256,1536]{1,0:T(8,128)(2,1)}, u32[]{:S(2)}, u32[]{:S(2)}) collective-permute-start(bf16[256,1536]{1,0:T(8,128)(2,1)} %relay.9.refs_9_), channel_id=1, source_target_pairs={{0,2},{2,0},{1,3},{3,1},{4,6},{6,4},{5,7},{7,5},{8,10},{10,8},{9,1... | collective-permute-start | bytes 2359304 | tf_op jit(solution)/shard_map/ppermute | solution.py:43
  90.4 32.3 %collective-permute-start.11 = (bf16[512,192]{1,0:T(8,128)(2,1)}, bf16[512,192]{1,0:T(8,128)(2,1)}, u32[]{:S(2)}, u32[]{:S(2)}) collective-permute-start(bf16[512,192]{1,0:T(8,128)(2,1)} %collective-permute-done.9.refs_2_.refs_1_.refs_5_), channel_id=1, source_target_pairs={{0,2},{2,0},{1,3},{3,1},{4,6},{6,4},{5,7},{7,5},{8,10},{10,8},{9,1... | collective-permute-start | bytes 589832 | tf_op jit(solution)/shard_map/ppermute | solution.py:43
  135.9 50.0 %collective-permute-start.24 = (bf16[256,1536]{1,0:T(8,128)(2,1)}, bf16[256,1536]{1,0:T(8,128)(2,1)}, u32[]{:S(2)}, u32[]{:S(2)}) collective-permute-start(bf16[256,1536]{1,0:T(8,128)(2,1)} %pass_on.6.refs_9_), channel_id=1, source_target_pairs={{0,2},{2,0},{1,3},{3,1},{4,6},{6,4},{5,7},{7,5},{8,10},{10,8},{9,1... | collective-permute-start | bytes 2359304 | tf_op jit(solution)/shard_map/ppermute | solution.py:43
  181.3 42.9 %collective-permute-start.23 = (bf16[4,192,992]{2,1,0:T(8,128)(2,1)}, bf16[4,192,992]{2,1,0:T(8,128)(2,1)}, u32[]{:S(2)}, u32[]{:S(2)}) collective-permute-start(bf16[4,192,992]{2,1,0:T(8,128)(2,1)} %get-tuple-element.136), channel_id=1, source_target_pairs={{0,4},{4,0},{8,12},{12,8},{16,20},{20,16},{24,28},{28,24},{1,5},{5... | collective-permute-start | bytes 4571144 | tf_op jit(solution)/shard_map/ppermute | solution.py:601
  185.3 70.0 %collective-permute-start.28 = (bf16[256,1536]{1,0:T(8,128)(2,1)}, bf16[256,1536]{1,0:T(8,128)(2,1)}, u32[]{:S(2)}, u32[]{:S(2)}) collective-permute-start(bf16[256,1536]{1,0:T(8,128)(2,1)} %pass_on.7.refs_10_), channel_id=1, source_target_pairs={{0,2},{2,0},{1,3},{3,1},{4,6},{6,4},{5,7},{7,5},{8,10},{10,8},{9,1... | collective-permute-start | bytes 2359304 | tf_op jit(solution)/shard_map/ppermute | solution.py:43
  203.5 74.4 %collective-permute-start.32 = (bf16[4,192,992]{2,1,0:T(8,128)(2,1)}, bf16[4,192,992]{2,1,0:T(8,128)(2,1)}, u32[]{:S(2)}, u32[]{:S(2)}) collective-permute-start(bf16[4,192,992]{2,1,0:T(8,128)(2,1)} %get-tuple-element.159), channel_id=1, source_target_pairs={{0,8},{4,12},{8,0},{12,4},{16,24},{20,28},{24,16},{28,20},{1,9},{5... | collective-permute-start | bytes 4571144 | tf_op jit(solution)/shard_map/ppermute | solution.py:601
  230.8 37.1 %collective-permute-start.26 = (bf16[2,256,1536]{2,1,0:T(8,128)(2,1)}, bf16[2,256,1536]{2,1,0:T(8,128)(2,1)}, u32[]{:S(2)}, u32[]{:S(2)}) collective-permute-start(bf16[2,256,1536]{2,1,0:T(8,128)(2,1)} %pass_on.8.refs_13_), channel_id=1, source_target_pairs={{0,2},{2,0},{1,3},{3,1},{4,6},{6,4},{5,7},{7,5},{8,10},{10,8},{9,1... | collective-permute-start | bytes 4718600 | tf_op jit(solution)/shard_map/ppermute | solution.py:43
  231.4 41.7 %collective-permute-start.27 = (bf16[2,192,992]{2,1,0:T(8,128)(2,1)}, bf16[2,192,992]{2,1,0:T(8,128)(2,1)}, u32[]{:S(2)}, u32[]{:S(2)}) collective-permute-start(bf16[2,192,992]{2,1,0:T(8,128)(2,1)} %get-tuple-element.147), channel_id=1, source_target_pairs={{0,8},{4,12},{8,0},{12,4},{16,24},{20,28},{24,16},{28,20},{1,9},{5... | collective-permute-start | bytes 2285576 | tf_op jit(solution)/shard_map/ppermute | solution.py:601
  232.9 89.9 %collective-permute-start.38 = (bf16[4,192,992]{2,1,0:T(8,128)(2,1)}, bf16[4,192,992]{2,1,0:T(8,128)(2,1)}, u32[]{:S(2)}, u32[]{:S(2)}) collective-permute-start(bf16[4,192,992]{2,1,0:T(8,128)(2,1)} %get-tuple-element.172), channel_id=1, source_target_pairs={{0,4},{4,0},{8,12},{12,8},{16,20},{20,16},{24,28},{28,24},{1,5},{5... | collective-permute-start | bytes 4571144 | tf_op jit(solution)/shard_map/ppermute | solution.py:601
  255.4 27.9 %collective-permute-start.31 = (bf16[512,1536]{1,0:T(8,128)(2,1)}, bf16[512,1536]{1,0:T(8,128)(2,1)}, u32[]{:S(2)}, u32[]{:S(2)}) collective-permute-start(bf16[512,1536]{1,0:T(8,128)(2,1)} %get-tuple-element.158), channel_id=1, source_target_pairs={{0,1},{1,0},{2,3},{3,2},{4,5},{5,4},{6,7},{7,6},{8,9},{9,8},{10,11... | collective-permute-start | bytes 4718600 | tf_op jit(solution)/shard_map/ppermute | solution.py:47
  275.3 72.8 %collective-permute-start.30 = (bf16[1,192,992]{2,1,0:T(8,128)(2,1)}, bf16[1,192,992]{2,1,0:T(8,128)(2,1)}, u32[]{:S(2)}, u32[]{:S(2)}) collective-permute-start(bf16[1,192,992]{2,1,0:T(8,128)(2,1)} %get-tuple-element.154), channel_id=1, source_target_pairs={{0,16},{4,20},{8,24},{12,28},{16,0},{20,4},{24,8},{28,12},{1,17},{... | collective-permute-start | bytes 1142792 | tf_op jit(solution)/shard_map/ppermute | solution.py:601
  280.6 80.0 %collective-permute-start.42 = (bf16[2,192,992]{2,1,0:T(8,128)(2,1)}, bf16[2,192,992]{2,1,0:T(8,128)(2,1)}, u32[]{:S(2)}, u32[]{:S(2)}) collective-permute-start(bf16[2,192,992]{2,1,0:T(8,128)(2,1)} %get-tuple-element.182), channel_id=1, source_target_pairs={{0,16},{4,20},{8,24},{12,28},{16,0},{20,4},{24,8},{28,12},{1,17},{... | collective-permute-start | bytes 2285576 | tf_op jit(solution)/shard_map/ppermute | solution.py:601
  285.5 123.2 %collective-permute-start.40 = (bf16[256,1536]{1,0:T(8,128)(2,1)}, bf16[256,1536]{1,0:T(8,128)(2,1)}, u32[]{:S(2)}, u32[]{:S(2)}) collective-permute-start(bf16[256,1536]{1,0:T(8,128)(2,1)} %pass_on.9.refs_10_), channel_id=1, source_target_pairs={{0,2},{2,0},{1,3},{3,1},{4,6},{6,4},{5,7},{7,5},{8,10},{10,8},{9,1... | collective-permute-start | bytes 2359304 | tf_op jit(solution)/shard_map/ppermute | solution.py:43
  291.1 28.0 %collective-permute-start.34 = (bf16[2,192,1536]{2,1,0:T(8,128)(2,1)}, bf16[2,192,1536]{2,1,0:T(8,128)(2,1)}, u32[]{:S(2)}, u32[]{:S(2)}) collective-permute-start(bf16[2,192,1536]{2,1,0:T(8,128)(2,1)} %get-tuple-element.163), channel_id=1, source_target_pairs={{0,1},{1,0},{2,3},{3,2},{4,5},{5,4},{6,7},{7,6},{8,9},{9,8},{10,11... | collective-permute-start | bytes 3538952 | tf_op jit(solution)/shard_map/ppermute | solution.py:47
  367.0 49.2 %collective-permute-start.39 = (bf16[256,1536]{1,0:T(8,128)(2,1)}, bf16[256,1536]{1,0:T(8,128)(2,1)}, u32[]{:S(2)}, u32[]{:S(2)}) collective-permute-start(bf16[256,1536]{1,0:T(8,128)(2,1)} %pass_on.11.refs_8_), channel_id=1, source_target_pairs={{0,2},{2,0},{1,3},{3,1},{4,6},{6,4},{5,7},{7,5},{8,10},{10,8},{9,1... | collective-permute-start | bytes 2359304 | tf_op jit(solution)/shard_map/ppermute | solution.py:43
  367.6 32.4 %collective-permute-start.47 = (bf16[4,192,768]{2,1,0:T(8,128)(2,1)}, bf16[4,192,768]{2,1,0:T(8,128)(2,1)}, u32[]{:S(2)}, u32[]{:S(2)}) collective-permute-start(bf16[4,192,768]{2,1,0:T(8,128)(2,1)} %get-tuple-element.186), channel_id=1, source_target_pairs={{0,4},{4,0},{8,12},{12,8},{16,20},{20,16},{24,28},{28,24},{1,5},{5... | collective-permute-start | bytes 3538952 | tf_op jit(solution)/shard_map/ppermute | solution.py:601
  406.5 33.1 %collective-permute-start.48 = (f32[1,3456]{1,0:T(1,128)}, f32[1,3456]{1,0:T(1,128)}, u32[]{:S(2)}, u32[]{:S(2)}) collective-permute-start(f32[1,3456]{1,0:T(1,128)} %small_sum.3.refs_7_.refs_0_), channel_id=1, source_target_pairs={{0,4},{4,0},{8,12},{12,8},{16,20},{20,16},{24,28},{28,24},{1,5},{5... | collective-permute-start | bytes 41480 | tf_op jit(solution)/shard_map/ppermute | solution.py:777
  407.1 32.4 %collective-permute-start.49 = (f32[1,3456]{1,0:T(1,128)}, f32[1,3456]{1,0:T(1,128)}, u32[]{:S(2)}, u32[]{:S(2)}) collective-permute-start(f32[1,3456]{1,0:T(1,128)} %small_sum.3.refs_7_.refs_0_), channel_id=1, source_target_pairs={{0,8},{4,12},{8,0},{12,4},{16,24},{20,28},{24,16},{28,20},{1,9},{5... | collective-permute-start | bytes 41480 | tf_op jit(solution)/shard_map/ppermute | solution.py:777
  408.7 30.8 %collective-permute-start.50 = (f32[1,3456]{1,0:T(1,128)}, f32[1,3456]{1,0:T(1,128)}, u32[]{:S(2)}, u32[]{:S(2)}) collective-permute-start(f32[1,3456]{1,0:T(1,128)} %small_sum.3.refs_7_.refs_0_), channel_id=1, source_target_pairs={{0,12},{4,8},{8,4},{12,0},{16,28},{20,24},{24,20},{28,16},{1,13},{... | collective-permute-start | bytes 41480 | tf_op jit(solution)/shard_map/ppermute | solution.py:777
  (132 other events, 1334.2 us)
